TPU v7x, 32 devices: a whole 2x2x4 slice. The times are simulated.
32 devices in a mesh: replica: 2 (over y), tensor: 4 (over z), adapter: 4 (over x, core).
Axes of the slice: x: 2, y: 2, z: 4, core: 2. Of those that a mesh axis runs over, the one named last changes fastest.
Arguments:
- requests: bfloat16 [3072, 8192], P(('replica', 'adapter'), 'tensor'), parts along dimension 0, may hold values from -6 to 6
- query_weight: bfloat16 [8192, 8192], P(None, 'tensor'), may hold values from -0.0625 to 0.0625
- adapter_down_factor: bfloat16 [32, 64, 8192], P('adapter', None, 'tensor'), may hold values from -0.0625 to 0.0625
- adapter_up_factor: bfloat16 [32, 64, 8192], P('adapter', None, 'tensor'), may hold values from -0.75 to 0.75
- request_adapter_index: int32 [3072, 1], P(('replica', 'adapter')), parts along dimension 0, may hold values from 0 to 31; in each aligned block of 384 rows (0 to 383, 384 to 767, ...) at most 24 rows name the same one
Outputs:
- queries: bfloat16 [3072, 8192], P(('replica', 'adapter'), 'tensor'), parts along dimension 0
There are 2 independent parts, one for each index of `replica`. A program takes and returns all parts, laid end to end along the dimension named above; an argument that names none is the same for every part. Nothing has to cross between parts.
Inputs may be any that keep to these rules, and one draw needn't show every extreme that they name: `request_adapter_index`: among the 384 requests of one device (aligned blocks of rows), no adapter is named more than 24 times.
All inputs are finite; a program needn't handle non-finite values.
Results may differ from a plain program's by a relative error of at most 0.0075.
Values may be sent and summed in bfloat16 or wider, within the bound.
No kernel may reach another device: no remote copies, remote signals or barrier semaphores. Data moves between devices by JAX's collectives and lax.ppermute only.
A program may use at most 128 MiB of HBM per device.

v0:
```python
import jax
import jax.numpy as jnp
from jax import lax
from jax.sharding import PartitionSpec as P

adapter_scale = 0.5


def local(requests, query_weight, adapter_down_factor, adapter_up_factor, request_adapter_index):
    local_cols = query_weight.shape[1]
    row_count = requests.shape[0]
    features = requests.shape[1]
    base_query_output = jnp.dot(
        lax.all_gather(requests, "tensor", axis=1, tiled=True),
        query_weight,
        preferred_element_type=jnp.float32,
    )
    resident_adapters = adapter_down_factor.shape[0]
    groups = lax.axis_size("adapter")
    total_adapters = resident_adapters * groups
    capacity = max(2, 2 * row_count // total_adapters)
    slot_count = total_adapters * capacity
    adapter_of = request_adapter_index[:, 0]
    onehot = (adapter_of[:, None] == jnp.arange(total_adapters, dtype=jnp.int32)[None, :]).astype(
        jnp.float32
    )
    positions = jnp.arange(row_count, dtype=jnp.int32)
    earlier = (positions[None, :] < positions[:, None]).astype(jnp.float32)
    before = jnp.dot(
        earlier, onehot, preferred_element_type=jnp.float32, precision=lax.Precision.HIGHEST
    )
    order_in = jnp.sum(before * onehot, axis=1).astype(jnp.int32)
    slot_index = adapter_of * capacity + order_in
    placer = (slot_index[:, None] == jnp.arange(slot_count, dtype=jnp.int32)[None, :]).astype(
        jnp.bfloat16
    )
    slotted = jnp.einsum("rs,rd->sd", placer, requests, preferred_element_type=jnp.float32).astype(
        jnp.bfloat16
    )
    down_all, up_all = (
        lax.all_gather(adapter_down_factor, "adapter", axis=0, tiled=True),
        lax.all_gather(adapter_up_factor, "adapter", axis=0, tiled=True),
    )
    grouped = slotted.reshape(total_adapters, capacity, features)
    partial_rank = jnp.einsum("akd,ard->akr", grouped, down_all, preferred_element_type=jnp.float32)
    reduced = lax.psum(partial_rank.astype(jnp.bfloat16), "tensor")
    lifted = jnp.einsum("akr,arc->akc", reduced, up_all, preferred_element_type=jnp.float32).astype(
        jnp.bfloat16
    )
    adapter_corrections = lifted.reshape(slot_count, local_cols)
    scatter_layout = jnp.einsum(
        "rs,sc->rc", placer, adapter_corrections, preferred_element_type=jnp.float32
    )
    return (base_query_output + adapter_scale * scatter_layout).astype(jnp.bfloat16)


def solution(mesh):
    placed = (
        P(("replica", "adapter"), "tensor"),
        P(None, "tensor"),
        P("adapter", None, "tensor"),
        P("adapter", None, "tensor"),
        P(("replica", "adapter"), None),
    )
    return jax.shard_map(
        local,
        mesh=mesh,
        in_specs=placed,
        out_specs=P(("replica", "adapter"), "tensor"),
        check_vma=False,
    )
```

profile of v0, /device:TPU:0, one launch (start us, length us, event | category | flops | bytes accessed | tf_op | source)
XLA Modules:
  0.0 295.9 jit_solution(13346218732736876261)
XLA Ops:
  6.5 0.0 copy-start
  6.5 0.0 all-gather.6.cloned.1.call-start
  6.5 0.7 all-gather.6.cloned.1.call-update
  7.3 0.0 all-gather.4.cloned.1.call-start
  7.3 0.7 all-gather.4.cloned.1.call-update
  8.0 0.0 all-gather.8.cloned.1.call-start
  8.1 0.7 all-gather.8.cloned.1.call-update
  8.7 0.0 all-reduce.2.cloned.1.call-start
  8.8 0.0 copy-done
  8.8 0.2 fusion
  9.1 3.3 %convolution_convert_fusion.1 = bf16[768,2048]{1,0:T(8,128)(2,1)S(1)} fusion(bf16[384,2048]{1,0:T(8,128)(2,1)} %param.5, s32[384]{0:T(512)S(1)} %add_reduce_fusion), kind=kOutput, calls=%fused_computation.1 | convolution fusion | flops 1209827328 | bytes 4720128 | tf_op jit(solution)/shard_map/rs,rd->sd/dot_general | solution.py:37
  12.4 57.5 %all-gather.6.cloned.1.call-done = bf16[32,64,2048]{2,1,0:T(8,128)(2,1)} async-done(((bf16[8,64,2048]{2,1,0:T(8,128)(2,1)}), bf16[32,64,2048]{2,1,0:T(8,128)(2,1)}) %all-gather.6.cloned.1.call-update) | async-done | bytes 8388624 | tf_op jit(solution)/shard_map/all_gather | solution.py:41
  69.9 6.4 %convolution_convert_fusion.2 = bf16[32,24,64]{2,1,0:T(8,128)(2,1)} fusion(bf16[32,24,2048]{2,1,0:T(8,128)(2,1)S(1)} %bitcast.11, bf16[32,64,2048]{2,1,0:T(8,128)(2,1)} %all-gather.6.cloned.1.call-done), kind=kOutput, calls=%fused_computation.4 | convolution fusion | flops 201375744 | bytes 11632640 | tf_op jit(solution)/shard_map/akd,ard->akr/dot_general | solution.py:45
  76.3 0.0 all-reduce.2.cloned.1.call-update
  76.3 110.6 %all-gather.4.cloned.1.call-done = bf16[384,8192]{1,0:T(8,128)(2,1)} async-done(((bf16[384,2048]{1,0:T(8,128)(2,1)}), bf16[384,8192]{1,0:T(8,128)(2,1)}) %all-gather.4.cloned.1.call-update) | async-done | bytes 6291472 | tf_op jit(solution)/shard_map/all_gather | solution.py:14
  186.9 20.4 %fusion.4 = f32[384,2048]{1,0:T(8,128)S(1)} fusion(bf16[384,8192]{1,0:T(8,128)(2,1)} %all-gather.4.cloned.1.call-done, bf16[8192,2048]{1,0:T(8,128)(2,1)} %param.6), kind=kOutput, calls=%fused_computation.13 | convolution fusion | flops 12884901888 | bytes 42991616 | tf_op jit(solution)/shard_map/dot_general | solution.py:13
  207.3 37.7 %all-gather.8.cloned.1.call-done = bf16[32,64,2048]{2,1,0:T(8,128)(2,1)} async-done(((bf16[8,64,2048]{2,1,0:T(8,128)(2,1)}), bf16[32,64,2048]{2,1,0:T(8,128)(2,1)}) %all-gather.8.cloned.1.call-update) | async-done | bytes 8388624 | tf_op jit(solution)/shard_map/all_gather | solution.py:42
  245.0 37.0 %all-reduce.2.cloned.1.call-done = bf16[32,24,64]{2,1,0:T(8,128)(2,1)} async-done(((bf16[32,24,64]{2,1,0:T(8,128)(2,1)}), bf16[32,24,64]{2,1,0:T(8,128)(2,1)}) %all-reduce.2.cloned.1.call-update) | async-done | bytes 98320 | tf_op jit(solution)/shard_map/psum | solution.py:46
  282.0 4.7 %convolution_convert_fusion = bf16[32,24,2048]{2,1,0:T(8,128)(2,1)S(1)} fusion(bf16[32,24,64]{2,1,0:T(8,128)(2,1)} %all-reduce.2.cloned.1.call-done, bf16[32,64,2048]{2,1,0:T(8,128)(2,1)} %all-gather.8.cloned.1.call-done), kind=kOutput, calls=%fused_computation | convolution fusion | flops 202899456 | bytes 11632640 | tf_op jit(solution)/shard_map/akr,arc->akc/dot_general | solution.py:47
  286.7 2.7 add_convert_fusion
  (3 shorter events, 0.0 us)
Async XLA Ops:
  6.5 2.3 copy-start
  6.5 63.4 %all-gather.6.cloned.1.call-start = ((), (), s32[]{:S(2)}) async-start(), calls=%async_computation.1 | async-start | bytes 10485760 | tf_op jit(solution)/shard_map/all_gather | solution.py:41
  7.3 179.6 %all-gather.4.cloned.1.call-start = ((), (), s32[]{:S(2)}) async-start(), calls=%async_computation | async-start | bytes 7864320 | tf_op jit(solution)/shard_map/all_gather | solution.py:14
  8.0 237.0 %all-gather.8.cloned.1.call-start = ((), (), s32[]{:S(2)}) async-start(), calls=%async_computation.3 | async-start | bytes 10485760 | tf_op jit(solution)/shard_map/all_gather | solution.py:42
  8.7 273.3 %all-reduce.2.cloned.1.call-start = ((), (), s32[]{:S(2)}) async-start(), calls=%async_computation.2 | async-start | bytes 393216 | tf_op jit(solution)/shard_map/psum | solution.py:46
Sparse Core Ops, SparseCore 0:
  8.9 60.9 all-gather.5
  71.5 115.3 all-gather.3
  188.5 56.4 all-gather.7
  247.1 34.8 all-reduce.1
where the time goes:
time: 296 us
  waiting for transfers between devices  245 us (83%)
  matrix products  37.6 us (13%)
  between operations  13.2 us (4%)
    all_gather x1, waiting for transfers between devices, local(): lax.all_gather(requests, 'tensor', axis=1, tiled=True)  111 us
    all_gather x1, waiting for transfers between devices, local(): lax.all_gather(adapter_down_factor, 'adapter', axis=0, tiled=True)  57.5 us
    all_gather x1, waiting for transfers between devices, local(): lax.all_gather(adapter_up_factor, 'adapter', axis=0, tiled=True)  37.7 us
    psum x1, waiting for transfers between devices, local(): reduced = lax.psum(partial_rank.astype(jnp.bfloat16), 'tensor')  37 us
    dot_general x1, matrix products, local(): jnp.dot(lax.all_gather(requests, 'tensor', axis=1, tiled=True), query_wei...  20.4 us
    dot_general x1, matrix products, local(): jnp.einsum('akd,ard->akr', grouped, down_all, preferred_element_type=jnp....  6.36 us
  transfers between devices with their start and end apart: 4, of which 4 were waited for; matrix products, arithmetic and copies ran while one was open for 10% of the time, Pallas kernels for 0%

commit v1 on v0

v1 whole, which is shorter than its diff:
```python
import jax
import jax.numpy as jnp
from jax import lax
from jax.sharding import PartitionSpec as P

adapter_scale = 0.5
CHUNKS = 2


def rank_spread(count, rank):
    rows = lax.broadcasted_iota(jnp.int32, (count * rank, rank), 0)
    cols = lax.broadcasted_iota(jnp.int32, (count * rank, rank), 1)
    return (rows % rank == cols).astype(jnp.bfloat16)


def owner_mask(adapter_of, first, count, rank):
    cols = lax.broadcasted_iota(jnp.int32, (1, count * rank), 1) // rank + first
    return adapter_of == cols


def gathered_factor(factor, order):
    resident, rank, width = factor.shape
    groups = lax.axis_size("adapter")
    me = lax.axis_index("adapter")
    flat = factor.reshape(resident * rank, width)
    copies = lax.axis_size("replica")
    if groups != 4 or copies != 2:
        whole = lax.all_gather(flat, "adapter", axis=0, tiled=True)
        return [(whole, jnp.int32(0))]
    half = resident * rank // 2
    mine = lax.axis_index("replica")
    across = [(0, 2), (2, 0), (1, 3), (3, 1)]
    beside = [(0, 1), (1, 0), (2, 3), (3, 2)]
    sent = lax.dynamic_slice_in_dim(flat, mine * half, half, 0)
    far_mine = lax.ppermute(sent, "adapter", across)
    far_other = lax.ppermute(far_mine, "replica", [(0, 1), (1, 0)])
    near = lax.ppermute(flat, "adapter", beside)
    near_mine = lax.ppermute(far_mine, "adapter", beside)
    near_other = lax.ppermute(far_other, "adapter", beside)
    h = resident // 2
    return [
        (flat, me * resident),
        (near, (me ^ 1) * resident),
        (far_mine, (me ^ 2) * resident + mine * h),
        (near_mine, (me ^ 3) * resident + mine * h),
        (far_other, (me ^ 2) * resident + (1 - mine) * h),
        (near_other, (me ^ 3) * resident + (1 - mine) * h),
    ]


def local(requests, query_weight, adapter_down_factor, adapter_up_factor, request_adapter_index):
    features = requests.shape[1]
    rank = adapter_down_factor.shape[1]
    spans = lax.axis_size("tensor")
    z = lax.axis_index("tensor")

    def base(block, owner, chunk, width):
        rows = lax.dynamic_slice_in_dim(query_weight, owner * features + chunk * width, width, 0)
        return jnp.dot(block, rows, preferred_element_type=jnp.float32)

    down = gathered_factor(adapter_down_factor, 0)
    up = gathered_factor(adapter_up_factor, 1)

    low = 0.0
    for piece, first in down:
        count = piece.shape[0] // rank
        full = lax.dot_general(
            requests, piece, (((1,), (1,)), ((), ())), preferred_element_type=jnp.float32
        )
        kept = jnp.where(owner_mask(request_adapter_index, first, count, rank), full, 0.0)
        low += jnp.dot(
            kept.astype(jnp.bfloat16), rank_spread(count, rank), preferred_element_type=jnp.float32
        )
    low = low.astype(jnp.bfloat16)

    if spans == 4:
        total = low.astype(jnp.float32)
        for bit in (1, 2, 3):
            total += lax.ppermute(low, "tensor", [(i, i ^ bit) for i in range(4)]).astype(
                jnp.float32
            )
        low = total.astype(jnp.bfloat16)
        width = features // CHUNKS
        pair = [(0, 1), (1, 0), (2, 3), (3, 2)]
        middle = [(1, 2), (2, 1)]
        outward = [(1, 0), (2, 3)]
        inner = (z == 1) | (z == 2)
        acc = base(requests, z, 0, features)
        for c in range(CHUNKS):
            x = requests[:, c * width : (c + 1) * width]
            a1 = lax.ppermute(x, "tensor", pair)
            m1 = lax.ppermute(x, "tensor", middle)
            m2 = lax.ppermute(a1, "tensor", middle)
            e2 = lax.ppermute(m1, "tensor", outward)
            e3 = lax.ppermute(m2, "tensor", outward)
            acc += base(a1, z ^ 1, c, width)
            acc += base(jnp.where(inner, m1, e2), jnp.where(inner, z ^ 3, z ^ 2), c, width)
            acc += base(jnp.where(inner, m2, e3), jnp.where(inner, z ^ 2, z ^ 3), c, width)
    else:
        low = lax.psum(low, "tensor")
        acc = jnp.dot(
            lax.all_gather(requests, "tensor", axis=1, tiled=True),
            query_weight,
            preferred_element_type=jnp.float32,
        )

    for piece, first in up:
        count = piece.shape[0] // rank
        spread = lax.dot_general(
            low * jnp.bfloat16(adapter_scale),
            rank_spread(count, rank),
            (((1,), (1,)), ((), ())),
            preferred_element_type=jnp.float32,
        ).astype(jnp.bfloat16)
        kept = jnp.where(owner_mask(request_adapter_index, first, count, rank), spread, 0)
        acc += jnp.dot(kept, piece, preferred_element_type=jnp.float32)
    return acc.astype(jnp.bfloat16)


def solution(mesh):
    placed = (
        P(("replica", "adapter"), "tensor"),
        P(None, "tensor"),
        P("adapter", None, "tensor"),
        P("adapter", None, "tensor"),
        P(("replica", "adapter"), None),
    )
    return jax.shard_map(
        local,
        mesh=mesh,
        in_specs=placed,
        out_specs=P(("replica", "adapter"), "tensor"),
        check_vma=False,
    )
```

time: 296 us -> 168 us (0.57)
  waiting for transfers between devices: 245 us -> 36.4 us
  matrix products: 37.6 us -> 88.7 us
  starting transfers between devices: 0.12 us -> 32.1 us
  between operations: 13.2 us -> 0.24 us
  local copies, waits for them, and re-layouts: 0.01 us -> 9.69 us
    all_gather x3 -> x0, waiting for transfers between devices: 206 us -> none  [the longest x1 111 us: local(): lax.all_gather(requests, 'tensor', axis=1, tiled=True)]
    dot_general x6 -> x21, matrix products: 37.6 us -> 88.7 us  [the longest x7 47.1 us: base(): return jnp.dot(block, rows, preferred_element_type=jnp.float32)]
    psum x1 -> x0, waiting for transfers between devices: 37 us -> none  [local(): reduced = lax.psum(partial_rank.astype(jnp.bfloat16), 'tensor')]
    ppermute x0 -> x23, waiting for transfers between devices: none -> 36.4 us  [the longest x2 15.2 us: local(): e2 = lax.ppermute(m1, 'tensor', outward)]
    ppermute x0 -> x23, starting transfers between devices: none -> 32.1 us  [the longest x2 7.54 us: local(): a1 = lax.ppermute(x, 'tensor', pair)]
    dynamic_slice x0 -> x2, local copies, waits for them, and re-layouts: none -> 4.6 us  [gathered_factor(): sent = lax.dynamic_slice_in_dim(flat, mine * half, half, 0)]
  transfers between devices with their start and end apart: 4 -> 23, of which waited for: 4 -> 5; matrix products, arithmetic and copies ran while one was open for 10% -> 48% of each run, Pallas kernels for 0% -> 0%
where the time goes in v1:
time: 168 us; the launch traced here: 167 us
  matrix products  88.7 us (53%)
  waiting for transfers between devices  36.4 us (22%)
  starting transfers between devices  32.1 us (19%)
  local copies, waits for them, and re-layouts  9.69 us (6%)
    dot_general x7, matrix products, base(): return jnp.dot(block, rows, preferred_element_type=jnp.float32)  47.1 us
    dot_general x6, matrix products, local(): acc += jnp.dot(kept, piece, preferred_element_type=jnp.float32)  26.8 us
    ppermute x2, waiting for transfers between devices, local(): e2 = lax.ppermute(m1, 'tensor', outward)  15.2 us
    ppermute x2, waiting for transfers between devices, local(): e3 = lax.ppermute(m2, 'tensor', outward)  14.5 us
    dot_general x6, matrix products, local(): jnp.dot(kept.astype(jnp.bfloat16), rank_spread(count, rank), preferred_el...  13.8 us
    ppermute x2, starting transfers between devices, local(): a1 = lax.ppermute(x, 'tensor', pair)  7.54 us
    ppermute x2, waiting for transfers between devices, local(): a1 = lax.ppermute(x, 'tensor', pair)  6.62 us
    ppermute x3, starting transfers between devices, local(): lax.ppermute(low, 'tensor', [(i, i ^ bit) for i in range(4)])  5.68 us
  transfers between devices with their start and end apart: 23, of which 5 were waited for; matrix products, arithmetic and copies ran while one was open for 48% of the time, Pallas kernels for 0%

profile of v1, /device:TPU:0, one launch (start us, length us, event | category | flops | bytes accessed | tf_op | source)
XLA Modules:
  0.0 167.2 jit_solution(10566484946412846430)
XLA Ops:
  0.0 2.5 %fusion.155 = (bf16[384,1024]{1,0:T(8,128)(2,1)}, bf16[384,1024]{1,0:T(8,128)(2,1)S(1)}) fusion(bf16[384,2048]{1,0:T(8,128)(2,1)} %param.5), kind=kLoop, calls=%fused_computation.189 | loop fusion | bytes 3145728 | tf_op jit(solution)/shard_map/slice | solution.py:90
  4.1 5.0 %collective-permute-start.5 = (bf16[384,1024]{1,0:T(8,128)(2,1)S(1)}, bf16[384,1024]{1,0:T(8,128)(2,1)}, u32[]{:S(2)}, u32[]{:S(2)}) collective-permute-start(bf16[384,1024]{1,0:T(8,128)(2,1)S(1)} %get-tuple-element.6), channel_id=1, source_target_pairs={{0,4},{4,0},{8,12},{12,8},{1,5},{5,1},{9,13},{13,9},{2,6},{6,2},{1... | collective-permute-start | bytes 2359304 | tf_op jit(solution)/shard_map/ppermute | solution.py:91
  9.1 2.3 %constant_dynamic-slice_fusion.1 = bf16[256,2048]{1,0:T(8,128)(2,1)} fusion(bf16[512,2048]{1,0:T(8,128)(2,1)} %bitcast.94, s32[]{:T(128)S(6)} %select_n.207), kind=kLoop, calls=%fused_computation.153 | loop fusion | bytes 2097156 | tf_op jit(solution)/shard_map/dynamic_slice | solution.py:34
  14.5 8.6 %fusion = f32[2048,384]{1,0:T(8,128)} fusion(bf16[384,2048]{1,0:T(8,128)(2,1)S(1)} %copy-done, bf16[8192,2048]{1,0:T(8,128)(2,1)} %param.6, s32[]{:T(128)S(6)} %select_n.188), kind=kOutput, calls=%fused_computation | convolution fusion | flops 3221225472 | bytes 13107204 | tf_op jit(solution)/shard_map/dot_general | solution.py:59
  23.1 2.3 %constant_dynamic-slice_fusion = bf16[256,2048]{1,0:T(8,128)(2,1)} fusion(bf16[512,2048]{1,0:T(8,128)(2,1)} %bitcast.7, s32[]{:T(128)S(6)} %select_n.207), kind=kLoop, calls=%fused_computation.152 | loop fusion | bytes 2097156 | tf_op jit(solution)/shard_map/dynamic_slice | solution.py:34
  25.4 2.5 %collective-permute-start = (bf16[384,1024]{1,0:T(8,128)(2,1)}, bf16[384,1024]{1,0:T(8,128)(2,1)}, u32[]{:S(2)}, u32[]{:S(2)}) collective-permute-start(bf16[384,1024]{1,0:T(8,128)(2,1)} %get-tuple-element.5), channel_id=1, source_target_pairs={{0,4},{4,0},{8,12},{12,8},{1,5},{5,1},{9,13},{13,9},{2,6},{6,2},{1... | collective-permute-start | bytes 2359304 | tf_op jit(solution)/shard_map/ppermute | solution.py:91
  28.0 2.8 %fusion.39 = f32[384,64]{0,1:T(8,128)S(1)} fusion(bf16[384,2048]{1,0:T(8,128)(2,1)S(1)} %copy-done, bf16[512,2048]{1,0:T(8,128)(2,1)} %bitcast.95, s32[512]{0:T(512)S(1)} %fusion.138, s32[384]{0:T(512)S(1)} %reduce, s32[512]{0:T(512)S(1)} %get-tuple-element.11, s32[512]{0:T(512)S(1)} %get-tuple-element.12, pred[512]{0:T(512)(128)(4,1)S(1)} %fusion.140), kind=kOutput, calls=%fused_computation.49 | convolution fusion | flops 831127552 | bytes 3776512 | tf_op jit(solution)/shard_map/dot_general | solution.py:71
  32.1 6.5 %fusion.6 = f32[2048,384]{1,0:T(8,128)} fusion(bf16[384,1024]{1,0:T(8,128)(2,1)} %collective-permute-done.5, bf16[8192,2048]{1,0:T(8,128)(2,1)} %param.6, s32[]{:T(128)S(6)} %select_n.197), kind=kOutput, calls=%fused_computation.6 | convolution fusion | flops 1610612736 | bytes 8126468 | tf_op jit(solution)/shard_map/dot_general | solution.py:59
  40.1 6.6 %collective-permute-done = bf16[384,1024]{1,0:T(8,128)(2,1)} collective-permute-done((bf16[384,1024]{1,0:T(8,128)(2,1)}, bf16[384,1024]{1,0:T(8,128)(2,1)}, u32[]{:S(2)}, u32[]{:S(2)}) %collective-permute-start) | collective-permute-done | bytes 786464 | tf_op jit(solution)/shard_map/ppermute | solution.py:91
  48.0 1.6 collective-permute-start.13
  49.6 6.5 %fusion.12 = f32[2048,384]{1,0:T(8,128)} fusion(bf16[384,1024]{1,0:T(8,128)(2,1)} %collective-permute-done, bf16[8192,2048]{1,0:T(8,128)(2,1)} %param.6, s32[]{:T(128)S(6)} %select_n.189), kind=kOutput, calls=%fused_computation.12 | convolution fusion | flops 1610612736 | bytes 8126468 | tf_op jit(solution)/shard_map/dot_general | solution.py:59
  56.1 7.3 %collective-permute-done.7 = bf16[384,1024]{1,0:T(8,128)(2,1)S(1)} collective-permute-done((bf16[384,1024]{1,0:T(8,128)(2,1)}, bf16[384,1024]{1,0:T(8,128)(2,1)S(1)}, u32[]{:S(2)}, u32[]{:S(2)}) %collective-permute-start.7) | collective-permute-done | bytes 786464 | tf_op jit(solution)/shard_map/ppermute | solution.py:94
  65.0 6.2 %fusion.4 = f32[384,2048]{0,1:T(8,128)} fusion(bf16[8192,2048]{1,0:T(8,128)(2,1)} %param.6, s32[]{:T(128)S(6)} %select_n.199, bf16[384,1024]{1,0:T(8,128)(2,1)} %collective-permute-done.6, bf16[384,1024]{1,0:T(8,128)(2,1)S(1)} %collective-permute-done.7, pred[]{:T(512)S(6)} %or.3), kind=kOutput, calls=%fused_computation.4 | convolution fusion | flops 1611005952 | bytes 8912901 | tf_op jit(solution)/shard_map/dot_general | solution.py:59
  71.2 7.9 %collective-permute-done.2 = bf16[384,1024]{1,0:T(8,128)(2,1)S(1)} collective-permute-done((bf16[384,1024]{1,0:T(8,128)(2,1)}, bf16[384,1024]{1,0:T(8,128)(2,1)S(1)}, u32[]{:S(2)}, u32[]{:S(2)}) %collective-permute-start.2) | collective-permute-done | bytes 786464 | tf_op jit(solution)/shard_map/ppermute | solution.py:94
  79.1 6.2 %fusion.10 = f32[384,2048]{0,1:T(8,128)} fusion(bf16[8192,2048]{1,0:T(8,128)(2,1)} %param.6, s32[]{:T(128)S(6)} %select_n.193, bf16[384,1024]{1,0:T(8,128)(2,1)} %collective-permute-done.1, bf16[384,1024]{1,0:T(8,128)(2,1)S(1)} %collective-permute-done.2, pred[]{:T(512)S(6)} %or.3), kind=kOutput, calls=%fused_computation.10 | convolution fusion | flops 1611005952 | bytes 8912901 | tf_op jit(solution)/shard_map/dot_general | solution.py:59
  85.3 1.6 collective-permute-start.3
  88.8 2.8 %fusion.44 = f32[384,64]{0,1:T(8,128)S(1)} fusion(f32[384,64]{0,1:T(8,128)S(1)} %fusion.39, bf16[384,2048]{1,0:T(8,128)(2,1)S(1)} %copy-done, bf16[512,2048]{1,0:T(8,128)(2,1)} %collective-permute-done.10, s32[512]{0:T(512)S(1)} %fusion.137, s32[384]{0:T(512)S(1)} %reduce, s32[512]{0:T(512)S(1)} %get-tuple-element.11, s32[512]{0:T(512)S(1)} %get-tuple-element.12, ...), kind=kOutput, calls=%fused_computation.54 | convolution fusion | flops 831152128 | bytes 3874816 | tf_op jit(solution)/shard_map/dot_general | solution.py:71
  91.5 2.1 %fusion.36 = f32[384,64]{0,1:T(8,128)S(1)} fusion(bf16[256,2048]{1,0:T(8,128)(2,1)} %collective-permute-done.13, bf16[384,2048]{1,0:T(8,128)(2,1)S(1)} %copy-done, s32[256]{0:T(256)S(1)} %get-tuple-element.7, s32[384]{0:T(512)S(1)} %reduce, s32[256]{0:T(256)S(1)} %get-tuple-element.9, s32[256]{0:T(256)S(1)} %get-tuple-element.10, ...), kind=kOutput, calls=%fused_computation.46 | convolution fusion | flops 415563776 | bytes 2724608 | tf_op jit(solution)/shard_map/dot_general | solution.py:71
  93.6 2.1 %fusion.42 = f32[384,64]{0,1:T(8,128)S(1)} fusion(f32[384,64]{0,1:T(8,128)S(1)} %fusion.44, bf16[256,2048]{1,0:T(8,128)(2,1)} %collective-permute-done.11, bf16[384,2048]{1,0:T(8,128)(2,1)S(1)} %copy-done, s32[256]{0:T(256)S(1)} %broadcast_add_fusion.3, s32[384]{0:T(512)S(1)} %reduce, s32[256]{0:T(256)S(1)} %get-tuple-element.9, ...), kind=kOutput, calls=%fused_computation.52 | convolution fusion | flops 415588352 | bytes 2822912 | tf_op jit(solution)/shard_map/dot_general | solution.py:71
  95.8 1.6 collective-permute-start.21
  98.9 2.1 %fusion.43 = f32[384,64]{0,1:T(8,128)S(1)} fusion(f32[384,64]{0,1:T(8,128)S(1)} %fusion.36, f32[384,64]{0,1:T(8,128)S(1)} %fusion.42, bf16[256,2048]{1,0:T(8,128)(2,1)} %collective-permute-done.12, bf16[384,2048]{1,0:T(8,128)(2,1)S(1)} %copy-done, s32[256]{0:T(256)S(1)} %get-tuple-element.8, s32[384]{0:T(512)S(1)} %reduce, s32[256]{0:T(256)S(1)} %get-tuple-element.9, ...), kind=kOutput, calls=%fused_computation.53 | convolution fusion | flops 415612928 | bytes 2921216 | tf_op jit(solution)/shard_map/dot_general | solution.py:71
  101.0 8.1 %collective-permute-done.9 = bf16[384,1024]{1,0:T(8,128)(2,1)} collective-permute-done((bf16[384,1024]{1,0:T(8,128)(2,1)}, bf16[384,1024]{1,0:T(8,128)(2,1)}, u32[]{:S(2)}, u32[]{:S(2)}) %collective-permute-start.9) | collective-permute-done | bytes 786464 | tf_op jit(solution)/shard_map/ppermute | solution.py:95
  109.0 6.5 %fusion.2 = f32[384,2048]{0,1:T(8,128)} fusion(bf16[8192,2048]{1,0:T(8,128)(2,1)} %param.6, s32[]{:T(128)S(6)} %select_n.201, bf16[384,1024]{1,0:T(8,128)(2,1)} %collective-permute-done.8, bf16[384,1024]{1,0:T(8,128)(2,1)} %collective-permute-done.9, pred[]{:T(512)S(6)} %or.3), kind=kOutput, calls=%fused_computation.2 | convolution fusion | flops 1611005952 | bytes 8912901 | tf_op jit(solution)/shard_map/dot_general | solution.py:59
  115.5 2.1 %fusion.45 = bf16[384,64]{0,1:T(8,128)(2,1)S(1)} fusion(f32[384,64]{0,1:T(8,128)S(1)} %fusion.43, bf16[256,2048]{1,0:T(8,128)(2,1)} %collective-permute-done.14, bf16[384,2048]{1,0:T(8,128)(2,1)S(1)} %copy-done, s32[256]{0:T(256)S(1)} %broadcast_add_fusion, s32[384]{0:T(512)S(1)} %reduce, s32[256]{0:T(256)S(1)} %get-tuple-element.9, ...), kind=kOutput, calls=%fused_computation.55 | convolution fusion | flops 415612928 | bytes 2773760 | tf_op jit(solution)/shard_map/dot_general | solution.py:71
  119.0 4.2 %collective-permute-start.16 = (bf16[384,64]{0,1:T(8,128)(2,1)S(1)}, bf16[384,64]{0,1:T(8,128)(2,1)S(1)}, u32[]{:S(2)}, u32[]{:S(2)}) collective-permute-start(bf16[384,64]{0,1:T(8,128)(2,1)S(1)} %fusion.45), channel_id=1, source_target_pairs={{0,8},{4,12},{8,0},{12,4},{1,9},{5,13},{9,1},{13,5},{2,10},{6,14},... | collective-permute-start | bytes 147464 | tf_op jit(solution)/shard_map/ppermute | solution.py:79
  123.3 6.5 %collective-permute-done.4 = bf16[384,1024]{1,0:T(8,128)(2,1)} collective-permute-done((bf16[384,1024]{1,0:T(8,128)(2,1)}, bf16[384,1024]{1,0:T(8,128)(2,1)}, u32[]{:S(2)}, u32[]{:S(2)}) %collective-permute-start.4) | collective-permute-done | bytes 786464 | tf_op jit(solution)/shard_map/ppermute | solution.py:95
  129.7 6.5 %fusion.8 = f32[384,2048]{0,1:T(8,128)} fusion(bf16[8192,2048]{1,0:T(8,128)(2,1)} %param.6, s32[]{:T(128)S(6)} %select_n.196, bf16[384,1024]{1,0:T(8,128)(2,1)} %collective-permute-done.3, bf16[384,1024]{1,0:T(8,128)(2,1)} %collective-permute-done.4, pred[]{:T(512)S(6)} %or.3), kind=kOutput, calls=%fused_computation.8 | convolution fusion | flops 1611005952 | bytes 8912901 | tf_op jit(solution)/shard_map/dot_general | solution.py:59
  137.7 2.0 %fusion.74 = f32[384,2048]{0,1:T(8,128)S(1)} fusion(bf16[256,2048]{1,0:T(8,128)(2,1)} %collective-permute-done.21, bf16[384,256]{1,0:T(8,128)(2,1)S(1)} %convolution_convert_fusion.1, s32[256]{0:T(256)S(1)} %get-tuple-element.7, s32[384]{0:T(512)S(1)} %reduce), kind=kOutput, calls=%fused_computation.91 | convolution fusion | flops 402849792 | bytes 4393472 | tf_op jit(solution)/shard_map/dot_general | solution.py:116
  141.4 4.6 %fusion.60 = f32[384,2048]{0,1:T(8,128)} fusion(bf16[512,2048]{1,0:T(8,128)(2,1)} %bitcast.7, bf16[384,512]{1,0:T(8,128)(2,1)S(1)} %convolution_convert_fusion, s32[512]{0:T(512)S(1)} %fusion.138, s32[384]{0:T(512)S(1)} %reduce), kind=kOutput, calls=%fused_computation.76 | convolution fusion | flops 805699584 | bytes 5639680 | tf_op jit(solution)/shard_map/dot_general | solution.py:116
  146.1 4.9 %fusion.61 = f32[384,2048]{0,1:T(8,128)} fusion(bf16[512,2048]{1,0:T(8,128)(2,1)} %collective-permute-done.18, bf16[384,512]{1,0:T(8,128)(2,1)S(1)} %convolution_convert_fusion, s32[512]{0:T(512)S(1)} %fusion.137, s32[384]{0:T(512)S(1)} %reduce), kind=kOutput, calls=%fused_computation.77 | convolution fusion | flops 805699584 | bytes 5639680 | tf_op jit(solution)/shard_map/dot_general | solution.py:116
  151.0 13.6 %fusion.22 = bf16[384,2048]{0,1:T(8,128)(2,1)} fusion(f32[384,2048]{0,1:T(8,128)S(1)} %fusion.74, f32[384,2048]{0,1:T(8,128)S(1)} %fusion.73, f32[384,2048]{0,1:T(8,128)S(1)} %fusion.72, f32[384,2048]{0,1:T(8,128)} %fusion.61, f32[384,2048]{0,1:T(8,128)} %fusion.60, f32[384,2048]{0,1:T(8,128)} %fusion.2, f32[384,2048]{0,1:T(8,128)} %fusion.4, ...), kind=kOutput, calls=%fused_computation.23 | convolution fusion | flops 413073408 | bytes 40569344 | tf_op jit(solution)/shard_map/dot_general | solution.py:116
  164.6 2.6 %copy.16 = bf16[384,2048]{1,0:T(8,128)(2,1)} copy(bf16[384,2048]{0,1:T(8,128)(2,1)} %fusion.22) | data formatting | bytes 3145728 | tf_op jit(solution)/shard_map/convert_element_type | solution.py:117
  (54 shorter events, 18.3 us)
Async XLA Ops:
  0.0 14.4 %copy-start = (bf16[384,2048]{1,0:T(8,128)(2,1)S(1)}, bf16[384,2048]{1,0:T(8,128)(2,1)}, u32[]{:S(2)}) copy-start(bf16[384,2048]{1,0:T(8,128)(2,1)} %param.5) | copy-start | bytes 4718596
  2.5 22.9 %collective-permute-start.6 = (bf16[384,1024]{1,0:T(8,128)(2,1)S(1)}, bf16[384,1024]{1,0:T(8,128)(2,1)}, u32[]{:S(2)}, u32[]{:S(2)}) collective-permute-start(bf16[384,1024]{1,0:T(8,128)(2,1)S(1)} %get-tuple-element.6), channel_id=1, source_target_pairs={{4,8},{8,4},{5,9},{9,5},{6,10},{10,6},{7,11},{11,7},{20,24},{24,20... | collective-permute-start | bytes 2359304 | tf_op jit(solution)/shard_map/ppermute | solution.py:92
  4.1 26.7 %collective-permute-start.5 = (bf16[384,1024]{1,0:T(8,128)(2,1)S(1)}, bf16[384,1024]{1,0:T(8,128)(2,1)}, u32[]{:S(2)}, u32[]{:S(2)}) collective-permute-start(bf16[384,1024]{1,0:T(8,128)(2,1)S(1)} %get-tuple-element.6), channel_id=1, source_target_pairs={{0,4},{4,0},{8,12},{12,8},{1,5},{5,1},{9,13},{13,9},{2,6},{6,2},{1... | collective-permute-start | bytes 2359304 | tf_op jit(solution)/shard_map/ppermute | solution.py:91
  9.1 79.1 %collective-permute-start.10 = (bf16[512,2048]{1,0:T(8,128)(2,1)}, bf16[512,2048]{1,0:T(8,128)(2,1)}, u32[]{:S(2)}, u32[]{:S(2)}) collective-permute-start(bf16[512,2048]{1,0:T(8,128)(2,1)} %bitcast.93), channel_id=1, source_target_pairs={{0,1},{1,0},{2,3},{3,2},{4,5},{5,4},{6,7},{7,6},{8,9},{9,8},{10,11... | collective-permute-start | bytes 6291464 | tf_op jit(solution)/shard_map/ppermute | solution.py:37
  11.4 36.6 %collective-permute-start.11 = (bf16[256,2048]{1,0:T(8,128)(2,1)}, bf16[256,2048]{1,0:T(8,128)(2,1)}, u32[]{:S(2)}, u32[]{:S(2)}) collective-permute-start(bf16[256,2048]{1,0:T(8,128)(2,1)} %constant_dynamic-slice_fusion.1), channel_id=1, source_target_pairs={{0,2},{2,0},{1,3},{3,1},{4,6},{6,4},{5,7},{7,5},{8,10},{10,8},{9,1... | collective-permute-start | bytes 3145736 | tf_op jit(solution)/shard_map/ppermute | solution.py:35
  12.9 25.7 %collective-permute-start.1 = (bf16[384,1024]{1,0:T(8,128)(2,1)}, bf16[384,1024]{1,0:T(8,128)(2,1)}, u32[]{:S(2)}, u32[]{:S(2)}) collective-permute-start(bf16[384,1024]{1,0:T(8,128)(2,1)} %get-tuple-element.5), channel_id=1, source_target_pairs={{4,8},{8,4},{5,9},{9,5},{6,10},{10,6},{7,11},{11,7},{20,24},{24,20... | collective-permute-start | bytes 2359304 | tf_op jit(solution)/shard_map/ppermute | solution.py:92
  14.5 13.5 %copy-start.1 = (s32[384,1]{0,1:T(1,128)S(1)}, s32[384,1]{0,1:T(1,128)}, u32[]{:S(2)}) copy-start(s32[384,1]{0,1:T(1,128)} %param.9) | copy-start | bytes 4612
  25.4 21.2 %collective-permute-start = (bf16[384,1024]{1,0:T(8,128)(2,1)}, bf16[384,1024]{1,0:T(8,128)(2,1)}, u32[]{:S(2)}, u32[]{:S(2)}) collective-permute-start(bf16[384,1024]{1,0:T(8,128)(2,1)} %get-tuple-element.5), channel_id=1, source_target_pairs={{0,4},{4,0},{8,12},{12,8},{1,5},{5,1},{9,13},{13,9},{2,6},{6,2},{1... | collective-permute-start | bytes 2359304 | tf_op jit(solution)/shard_map/ppermute | solution.py:91
  30.8 32.6 %collective-permute-start.7 = (bf16[384,1024]{1,0:T(8,128)(2,1)}, bf16[384,1024]{1,0:T(8,128)(2,1)S(1)}, u32[]{:S(2)}, u32[]{:S(2)}) collective-permute-start(bf16[384,1024]{1,0:T(8,128)(2,1)} %collective-permute-done.6), channel_id=1, source_target_pairs={{4,0},{8,12},{5,1},{9,13},{6,2},{10,14},{7,3},{11,15},{20,16},{24,... | collective-permute-start | bytes 2359304 | tf_op jit(solution)/shard_map/ppermute | solution.py:94
  38.6 57.1 %collective-permute-start.19 = (bf16[256,2048]{1,0:T(8,128)(2,1)}, bf16[256,2048]{1,0:T(8,128)(2,1)S(1)}, u32[]{:S(2)}, u32[]{:S(2)}) collective-permute-start(bf16[256,2048]{1,0:T(8,128)(2,1)} %constant_dynamic-slice_fusion), channel_id=1, source_target_pairs={{0,2},{2,0},{1,3},{3,1},{4,6},{6,4},{5,7},{7,5},{8,10},{10,8},{9,1... | collective-permute-start | bytes 3145736 | tf_op jit(solution)/shard_map/ppermute | solution.py:35
  46.7 32.4 %collective-permute-start.2 = (bf16[384,1024]{1,0:T(8,128)(2,1)}, bf16[384,1024]{1,0:T(8,128)(2,1)S(1)}, u32[]{:S(2)}, u32[]{:S(2)}) collective-permute-start(bf16[384,1024]{1,0:T(8,128)(2,1)} %collective-permute-done.1), channel_id=1, source_target_pairs={{4,0},{8,12},{5,1},{9,13},{6,2},{10,14},{7,3},{11,15},{20,16},{24,... | collective-permute-start | bytes 2359304 | tf_op jit(solution)/shard_map/ppermute | solution.py:94
  48.0 38.9 %collective-permute-start.13 = (bf16[256,2048]{1,0:T(8,128)(2,1)}, bf16[256,2048]{1,0:T(8,128)(2,1)}, u32[]{:S(2)}, u32[]{:S(2)}) collective-permute-start(bf16[256,2048]{1,0:T(8,128)(2,1)} %collective-permute-done.11), channel_id=1, source_target_pairs={{0,16},{16,0},{1,17},{17,1},{2,18},{18,2},{3,19},{19,3},{4,20},{20... | collective-permute-start | bytes 3145736 | tf_op jit(solution)/shard_map/ppermute | solution.py:36
  63.4 21.9 %collective-permute-start.8 = (bf16[384,1024]{1,0:T(8,128)(2,1)}, bf16[384,1024]{1,0:T(8,128)(2,1)}, u32[]{:S(2)}, u32[]{:S(2)}) collective-permute-start(bf16[384,1024]{1,0:T(8,128)(2,1)} %collective-permute-done.5), channel_id=1, source_target_pairs={{4,8},{8,4},{5,9},{9,5},{6,10},{10,6},{7,11},{11,7},{20,24},{24,20... | collective-permute-start | bytes 2359304 | tf_op jit(solution)/shard_map/ppermute | solution.py:93
  79.1 18.3 %collective-permute-start.12 = (bf16[256,2048]{1,0:T(8,128)(2,1)}, bf16[256,2048]{1,0:T(8,128)(2,1)}, u32[]{:S(2)}, u32[]{:S(2)}) collective-permute-start(bf16[256,2048]{1,0:T(8,128)(2,1)} %collective-permute-done.11), channel_id=1, source_target_pairs={{0,1},{1,0},{2,3},{3,2},{4,5},{5,4},{6,7},{7,6},{8,9},{9,8},{10,11... | collective-permute-start | bytes 3145736 | tf_op jit(solution)/shard_map/ppermute | solution.py:38
  85.3 10.5 %collective-permute-start.3 = (bf16[384,1024]{1,0:T(8,128)(2,1)}, bf16[384,1024]{1,0:T(8,128)(2,1)}, u32[]{:S(2)}, u32[]{:S(2)}) collective-permute-start(bf16[384,1024]{1,0:T(8,128)(2,1)} %collective-permute-done), channel_id=1, source_target_pairs={{4,8},{8,4},{5,9},{9,5},{6,10},{10,6},{7,11},{11,7},{20,24},{24,20... | collective-permute-start | bytes 2359304 | tf_op jit(solution)/shard_map/ppermute | solution.py:93
  86.9 22.2 %collective-permute-start.9 = (bf16[384,1024]{1,0:T(8,128)(2,1)}, bf16[384,1024]{1,0:T(8,128)(2,1)}, u32[]{:S(2)}, u32[]{:S(2)}) collective-permute-start(bf16[384,1024]{1,0:T(8,128)(2,1)} %collective-permute-done.8), channel_id=1, source_target_pairs={{4,0},{8,12},{5,1},{9,13},{6,2},{10,14},{7,3},{11,15},{20,16},{24,... | collective-permute-start | bytes 2359304 | tf_op jit(solution)/shard_map/ppermute | solution.py:95
  88.2 27.3 %collective-permute-start.14 = (bf16[256,2048]{1,0:T(8,128)(2,1)}, bf16[256,2048]{1,0:T(8,128)(2,1)}, u32[]{:S(2)}, u32[]{:S(2)}) collective-permute-start(bf16[256,2048]{1,0:T(8,128)(2,1)} %collective-permute-done.13), channel_id=1, source_target_pairs={{0,1},{1,0},{2,3},{3,2},{4,5},{5,4},{6,7},{7,6},{8,9},{9,8},{10,11... | collective-permute-start | bytes 3145736 | tf_op jit(solution)/shard_map/ppermute | solution.py:39
  95.7 50.4 %collective-permute-start.18 = (bf16[512,2048]{1,0:T(8,128)(2,1)}, bf16[512,2048]{1,0:T(8,128)(2,1)}, u32[]{:S(2)}, u32[]{:S(2)}) collective-permute-start(bf16[512,2048]{1,0:T(8,128)(2,1)} %bitcast.7), channel_id=1, source_target_pairs={{0,1},{1,0},{2,3},{3,2},{4,5},{5,4},{6,7},{7,6},{8,9},{9,8},{10,11... | collective-permute-start | bytes 6291464 | tf_op jit(solution)/shard_map/ppermute | solution.py:37
  95.8 40.5 %collective-permute-start.21 = (bf16[256,2048]{1,0:T(8,128)(2,1)S(1)}, bf16[256,2048]{1,0:T(8,128)(2,1)}, u32[]{:S(2)}, u32[]{:S(2)}) collective-permute-start(bf16[256,2048]{1,0:T(8,128)(2,1)S(1)} %collective-permute-done.19), channel_id=1, source_target_pairs={{0,16},{16,0},{1,17},{17,1},{2,18},{18,2},{3,19},{19,3},{4,20},{20... | collective-permute-start | bytes 3145736 | tf_op jit(solution)/shard_map/ppermute | solution.py:36
  97.4 32.4 %collective-permute-start.4 = (bf16[384,1024]{1,0:T(8,128)(2,1)}, bf16[384,1024]{1,0:T(8,128)(2,1)}, u32[]{:S(2)}, u32[]{:S(2)}) collective-permute-start(bf16[384,1024]{1,0:T(8,128)(2,1)} %collective-permute-done.3), channel_id=1, source_target_pairs={{4,0},{8,12},{5,1},{9,13},{6,2},{10,14},{7,3},{11,15},{20,16},{24,... | collective-permute-start | bytes 2359304 | tf_op jit(solution)/shard_map/ppermute | solution.py:95
  117.6 18.7 %collective-permute-start.17 = (bf16[384,64]{0,1:T(8,128)(2,1)S(1)}, bf16[384,64]{0,1:T(8,128)(2,1)S(1)}, u32[]{:S(2)}, u32[]{:S(2)}) collective-permute-start(bf16[384,64]{0,1:T(8,128)(2,1)S(1)} %fusion.45), channel_id=1, source_target_pairs={{0,12},{4,8},{8,4},{12,0},{1,13},{5,9},{9,5},{13,1},{2,14},{6,10},... | collective-permute-start | bytes 147464 | tf_op jit(solution)/shard_map/ppermute | solution.py:79
  119.0 17.8 %collective-permute-start.16 = (bf16[384,64]{0,1:T(8,128)(2,1)S(1)}, bf16[384,64]{0,1:T(8,128)(2,1)S(1)}, u32[]{:S(2)}, u32[]{:S(2)}) collective-permute-start(bf16[384,64]{0,1:T(8,128)(2,1)S(1)} %fusion.45), channel_id=1, source_target_pairs={{0,8},{4,12},{8,0},{12,4},{1,9},{5,13},{9,1},{13,5},{2,10},{6,14},... | collective-permute-start | bytes 147464 | tf_op jit(solution)/shard_map/ppermute | solution.py:79
  129.7 7.1 %collective-permute-start.15 = (bf16[384,64]{0,1:T(8,128)(2,1)S(1)}, bf16[384,64]{0,1:T(8,128)(2,1)S(1)}, u32[]{:S(2)}, u32[]{:S(2)}) collective-permute-start(bf16[384,64]{0,1:T(8,128)(2,1)S(1)} %fusion.45), channel_id=1, source_target_pairs={{0,4},{4,0},{8,12},{12,8},{1,5},{5,1},{9,13},{13,9},{2,6},{6,2},{1... | collective-permute-start | bytes 147464 | tf_op jit(solution)/shard_map/ppermute | solution.py:79
  136.3 4.3 %collective-permute-start.20 = (bf16[256,2048]{1,0:T(8,128)(2,1)S(1)}, bf16[256,2048]{1,0:T(8,128)(2,1)S(1)}, u32[]{:S(2)}, u32[]{:S(2)}) collective-permute-start(bf16[256,2048]{1,0:T(8,128)(2,1)S(1)} %collective-permute-done.19), channel_id=1, source_target_pairs={{0,1},{1,0},{2,3},{3,2},{4,5},{5,4},{6,7},{7,6},{8,9},{9,8},{10,11... | collective-permute-start | bytes 3145736 | tf_op jit(solution)/shard_map/ppermute | solution.py:38
  136.3 14.7 %collective-permute-start.22 = (bf16[256,2048]{1,0:T(8,128)(2,1)}, bf16[256,2048]{1,0:T(8,128)(2,1)}, u32[]{:S(2)}, u32[]{:S(2)}) collective-permute-start(bf16[256,2048]{1,0:T(8,128)(2,1)} %collective-permute-done.21), channel_id=1, source_target_pairs={{0,1},{1,0},{2,3},{3,2},{4,5},{5,4},{6,7},{7,6},{8,9},{9,8},{10,11... | collective-permute-start | bytes 3145736 | tf_op jit(solution)/shard_map/ppermute | solution.py:39

commit v2 on v0

v2 whole, which is shorter than its diff:
```python
import functools

import jax
import jax.numpy as jnp
from jax import lax
from jax.experimental import pallas as pl
from jax.experimental.pallas import tpu as pltpu
from jax.sharding import PartitionSpec as P

adapter_scale = 0.5
TILE = 512
TINY = 0.2
SHRINK = 0.2
FIRST = 0.2
def cost(rows, depth, cols, SHARE):
    return pl.CostEstimate(
        flops=1 + int(SHARE * 2 * rows * depth * cols),
        bytes_accessed=int(SHARE * (2 * depth * cols + 8 * rows * cols)),
        transcendentals=0,
    )


PARAMS = pltpu.CompilerParams(vmem_limit_bytes=28 * 2**20)


def rank_spread(count, rank):
    rows = lax.broadcasted_iota(jnp.int32, (count * rank, rank), 0)
    cols = lax.broadcasted_iota(jnp.int32, (count * rank, rank), 1)
    return (rows % rank == cols).astype(jnp.bfloat16)


def owner_mask(adapter_of, first, count, rank):
    cols = lax.broadcasted_iota(jnp.int32, (1, count * rank), 1) // rank + first
    return adapter_of == cols


def block_kernel(sizes, row_block, *refs):
    count = sum(sizes)
    xs, weight_ref, out_ref = refs[:count], refs[count], refs[-1]
    value = refs[count + 1][...] if len(refs) > count + 2 else 0.0
    at = i = 0
    for size in sizes:
        x = xs[i][...]
        for other in xs[i + 1 : i + size]:
            x += other[...]
        value += jnp.dot(
            x, weight_ref[at : at + x.shape[1], :], preferred_element_type=jnp.float32
        )
        at += x.shape[1]
        i += size
    out_ref[...] = value.astype(out_ref.dtype)


def add_block(acc, groups, weight, row_block, dtype=jnp.float32, share=TINY):
    rows = groups[0][0].shape[0]
    xs = [x for group in groups for x in group]
    depth = sum(group[0].shape[1] for group in groups)
    cols = weight.shape[1]
    specs = [pl.BlockSpec(x.shape, lambda n, b: (0, 0)) for x in xs]
    specs.append(pl.BlockSpec((depth, TILE), lambda n, b: (b[0], n)))
    tiles = pl.BlockSpec((rows, TILE), lambda n, b: (0, n))
    args = [row_block.astype(jnp.int32).reshape(1), *xs, weight]
    if acc is not None:
        specs.append(tiles)
        args.append(acc)
    return pl.pallas_call(
        functools.partial(block_kernel, tuple(len(group) for group in groups)),
        grid_spec=pltpu.PrefetchScalarGridSpec(
            num_scalar_prefetch=1, grid=(cols // TILE,), in_specs=specs, out_specs=tiles
        ),
        out_shape=jax.ShapeDtypeStruct((rows, cols), dtype),
        compiler_params=PARAMS,
        cost_estimate=cost(rows, depth, cols, share),
    )(*args)


def expand_kernel(counts, rank, firsts, low_ref, owner_ref, acc_ref, *rest):
    pieces, out_ref, spread_ref = rest[: len(counts)], rest[-2], rest[-1]

    @pl.when(pl.program_id(0) == 0)
    def _():
        at = 0
        for i, count in enumerate(counts):
            wide = lax.dot_general(
                low_ref[...],
                rank_spread(count, rank),
                (((1,), (1,)), ((), ())),
                preferred_element_type=jnp.float32,
            )
            kept = jnp.where(owner_mask(owner_ref[...], firsts[i], count, rank), wide, 0.0)
            spread_ref[:, at : at + count * rank] = kept.astype(jnp.bfloat16)
            at += count * rank

    total, at = 0.0, 0
    for i, count in enumerate(counts):
        total += jnp.dot(
            spread_ref[:, at : at + count * rank],
            pieces[i][...],
            preferred_element_type=jnp.float32,
        )
        at += count * rank
    out_ref[...] = acc_ref[...] + adapter_scale * total


def add_expanded(acc, low, owners, up, share=TINY):
    rows, cols = acc.shape
    rank = low.shape[1]
    counts = tuple(piece.shape[0] // rank for piece, _ in up)
    depth = sum(counts) * rank
    tiles = pl.BlockSpec((rows, TILE), lambda n, f: (0, n))
    return pl.pallas_call(
        functools.partial(expand_kernel, counts, rank),
        grid_spec=pltpu.PrefetchScalarGridSpec(
            num_scalar_prefetch=1,
            grid=(cols // TILE,),
            in_specs=[
                pl.BlockSpec((rows, rank), lambda n, f: (0, 0)),
                pl.BlockSpec((rows, 1), lambda n, f: (0, 0)),
                tiles,
            ]
            + [pl.BlockSpec((c * rank, TILE), lambda n, f: (0, n)) for c in counts],
            out_specs=tiles,
            scratch_shapes=[pltpu.VMEM((rows, depth), jnp.bfloat16)],
        ),
        out_shape=jax.ShapeDtypeStruct((rows, cols), jnp.float32),
        compiler_params=PARAMS,
        cost_estimate=cost(rows, depth, cols, share),
    )(jnp.stack([first for _, first in up]).astype(jnp.int32), low, owners, acc, *[p for p, _ in up])


ACROSS = [(0, 2), (2, 0), (1, 3), (3, 1)]
SWAP = [(0, 1), (1, 0)]
BESIDE = [(0, 1), (1, 0), (2, 3), (3, 2)]


def half_of(rows, which):
    half = rows.shape[0] // 2
    return lax.dynamic_slice_in_dim(rows, which * half, half, 0)


def shrink_kernel(count, rank, first, *refs):
    piece, xs, owners = refs[0], refs[1:3], refs[3:5]
    before, outs = refs[5:-2], refs[-2:]
    for i in range(2):
        full = lax.dot_general(
            xs[i][...], piece[...], (((1,), (1,)), ((), ())), preferred_element_type=jnp.float32
        )
        kept = jnp.where(owner_mask(owners[i][...], first[0], count, rank), full, 0.0)
        total = jnp.dot(
            kept.astype(jnp.bfloat16), rank_spread(count, rank), preferred_element_type=jnp.float32
        )
        outs[i][...] = total + before[i][...] if before else total


def add_shrunk(lows, piece, first, xs, owners, rank):
    rows, features = xs[0].shape
    whole = pl.BlockSpec(memory_space=pltpu.VMEM)
    args = [piece, *xs, *owners, *lows]
    return pl.pallas_call(
        functools.partial(shrink_kernel, piece.shape[0] // rank, rank),
        in_specs=[pl.BlockSpec(memory_space=pltpu.SMEM)] + [whole] * len(args),
        out_specs=[whole] * 2,
        out_shape=[jax.ShapeDtypeStruct((rows, rank), jnp.float32)] * 2,
        compiler_params=PARAMS,
        cost_estimate=cost(2 * rows, features, piece.shape[0], SHRINK),
    )(first.astype(jnp.int32).reshape(1), *args)


def local_line(requests, query_weight, adapter_down_factor, adapter_up_factor, owners):
    features = requests.shape[1]
    rank = adapter_down_factor.shape[1]
    z = lax.axis_index("tensor")
    inner = (z == 1) | (z == 2)

    me = lax.axis_index("adapter")
    replica = lax.axis_index("replica")
    resident = adapter_down_factor.shape[0]
    down = adapter_down_factor.reshape(resident * rank, features)
    up = adapter_up_factor.reshape(resident * rank, -1)

    pair, middle, outward = [(0, 1), (1, 0), (2, 3), (3, 2)], [(1, 2), (2, 1)], [(1, 0), (2, 3)]
    second, third = jnp.where(inner, z ^ 3, z ^ 2), jnp.where(inner, z ^ 2, z ^ 3)
    halves = [me * resident, (me ^ 2) * resident + replica * (resident // 2)]
    halves.append((me ^ 2) * resident + (1 - replica) * (resident // 2))

    a1 = lax.ppermute(requests, "tensor", pair)
    m1 = lax.ppermute(requests, "tensor", middle)
    acc = add_block(None, [[requests]], query_weight, z, share=FIRST)
    xs = (requests, lax.ppermute(requests, "adapter", BESIDE))
    both = (owners, lax.ppermute(owners, "adapter", BESIDE))
    down_mine = lax.ppermute(half_of(down, replica), "adapter", ACROSS)
    up_mine = lax.ppermute(half_of(up, replica), "adapter", ACROSS)
    lows = add_shrunk((), down, halves[0], xs, both, rank)
    down_mine, acc, lows = lax.optimization_barrier((down_mine, acc, lows))
    down_other = lax.ppermute(down_mine, "replica", SWAP)
    lows = add_shrunk(lows, down_mine, halves[1], xs, both, rank)
    a1, m1, lows = lax.optimization_barrier((a1, m1, lows))
    m2 = lax.ppermute(a1, "tensor", middle)
    e2 = lax.ppermute(m1, "tensor", outward)
    acc = add_block(acc, [[a1]], query_weight, z ^ 1)
    lows, acc = lax.optimization_barrier((lows, acc))
    lows = add_shrunk(lows, down_other, halves[2], xs, both, rank)
    low = lows[0] + lax.ppermute(lows[1].astype(jnp.bfloat16), "adapter", BESIDE).astype(jnp.float32)
    for bit in (1, 2):
        low = low.astype(jnp.bfloat16)
        low = low.astype(jnp.float32) + lax.ppermute(
            low, "tensor", [(i, i ^ bit) for i in range(4)]
        ).astype(jnp.float32)
    low = low.astype(jnp.bfloat16)
    m2, e2, low = lax.optimization_barrier((m2, e2, low))
    e3 = lax.ppermute(m2, "tensor", outward)

    up_other = lax.ppermute(up_mine, "replica", SWAP)
    up_other, _ = lax.optimization_barrier((up_other, m2))
    near = [lax.ppermute(piece, "adapter", BESIDE) for piece in (up, up_mine, up_other)]
    across = resident - 2 * (me % 2) * resident
    ups = list(zip((up, up_mine, up_other), halves)) + list(zip(near, [h + across for h in halves]))

    acc = add_block(acc, [[m1, e2]], query_weight, second)
    acc = add_expanded(acc, low, owners, ups)
    return add_block(acc, [[m2, e3]], query_weight, third, jnp.bfloat16)


def local_any(requests, query_weight, adapter_down_factor, adapter_up_factor, owners):
    rank, width = adapter_down_factor.shape[1:]
    down, up = (
        lax.all_gather(f, "adapter", axis=0, tiled=True).reshape(-1, width)
        for f in (adapter_down_factor, adapter_up_factor)
    )
    count = down.shape[0] // rank
    full = lax.dot_general(
        requests, down, (((1,), (1,)), ((), ())), preferred_element_type=jnp.float32
    )
    kept = jnp.where(owner_mask(owners, 0, count, rank), full, 0.0).astype(jnp.bfloat16)
    low = jnp.dot(kept, rank_spread(count, rank), preferred_element_type=jnp.float32)
    low = lax.psum(low.astype(jnp.bfloat16), "tensor")
    spread = lax.dot_general(
        low, rank_spread(count, rank), (((1,), (1,)), ((), ())), preferred_element_type=jnp.float32
    )
    kept = jnp.where(owner_mask(owners, 0, count, rank), spread, 0.0).astype(jnp.bfloat16)
    base = jnp.dot(
        lax.all_gather(requests, "tensor", axis=1, tiled=True),
        query_weight,
        preferred_element_type=jnp.float32,
    )
    delta = jnp.dot(kept, up, preferred_element_type=jnp.float32)
    return (base + adapter_scale * delta).astype(jnp.bfloat16)


def solution(mesh):
    placed = (
        P(("replica", "adapter"), "tensor"),
        P(None, "tensor"),
        P("adapter", None, "tensor"),
        P("adapter", None, "tensor"),
        P(("replica", "adapter"), None),
    )
    sizes = tuple(mesh.shape[axis] for axis in ("replica", "tensor", "adapter"))
    return jax.shard_map(
        local_line if sizes == (2, 4, 4) else local_any,
        mesh=mesh,
        in_specs=placed,
        out_specs=P(("replica", "adapter"), "tensor"),
        check_vma=False,
    )
```

time: 296 us -> 137 us (0.46)
  waiting for transfers between devices: 245 us -> 51.9 us
  Pallas kernels: 0 us -> 44.9 us
  matrix products: 37.6 us -> 0 us
  starting transfers between devices: 0.12 us -> 20.8 us
  local copies, waits for them, and re-layouts: 0.01 us -> 18 us
  between operations: 13.2 us -> 0.26 us
    all_gather x3 -> x0, waiting for transfers between devices: 206 us -> none  [the longest x1 111 us: local(): lax.all_gather(requests, 'tensor', axis=1, tiled=True)]
    ppermute x0 -> x17, waiting for transfers between devices: none -> 51.9 us  [the longest x2 24.4 us: local_line(): lax.ppermute(low, 'tensor', [(i, i ^ bit) for i in range(4)])]
    pallas_call x0 -> x8, Pallas kernels: none -> 44.9 us  [the longest x4 29.1 us: add_block(): pl.pallas_call(functools.partial(block_kernel, tuple((len(group) for grou...]
    dot_general x6 -> x0, matrix products: 37.6 us -> none  [the longest x1 20.4 us: local(): jnp.dot(lax.all_gather(requests, 'tensor', axis=1, tiled=True), query_wei...]
    psum x1 -> x0, waiting for transfers between devices: 37 us -> none  [local(): reduced = lax.psum(partial_rank.astype(jnp.bfloat16), 'tensor')]
    ppermute x0 -> x17, starting transfers between devices: none -> 20.8 us  [the longest x2 5.06 us: local_line(): lax.ppermute(low, 'tensor', [(i, i ^ bit) for i in range(4)])]
    unnamed x2 -> x31, local copies, waits for them, and re-layouts: 0.01 us -> 13.3 us
    dynamic_slice x0 -> x2, local copies, waits for them, and re-layouts: none -> 4.61 us  [half_of(): return lax.dynamic_slice_in_dim(rows, which * half, half, 0)]
  transfers between devices with their start and end apart: 4 -> 17, of which waited for: 4 -> 5; matrix products, arithmetic and copies ran while one was open for 10% -> 4% of each run, Pallas kernels for 0% -> 27%
where the time goes in v2:
time: 137 us; the launch traced here: 136 us
  waiting for transfers between devices  51.9 us (38%)
  Pallas kernels  44.9 us (33%)
  starting transfers between devices  20.8 us (15%)
  local copies, waits for them, and re-layouts  18 us (13%)
    pallas_call x4, Pallas kernels, add_block(): pl.pallas_call(functools.partial(block_kernel, tuple((len(group) for grou...  29.1 us
    ppermute x2, waiting for transfers between devices, local_line(): lax.ppermute(low, 'tensor', [(i, i ^ bit) for i in range(4)])  24.4 us
    ppermute x1, waiting for transfers between devices, local_line(): e3 = lax.ppermute(m2, 'tensor', outward)  16.8 us
    unnamed x31, local copies, waits for them, and re-layouts  13.3 us
    ppermute x1, waiting for transfers between devices, local_line(): down_mine = lax.ppermute(half_of(down, replica), 'adapter', ACROSS)  10.6 us
    pallas_call x3, Pallas kernels, add_shrunk(): pl.pallas_call(functools.partial(shrink_kernel, piece.shape[0] // rank, r...  8.67 us
    pallas_call x1, Pallas kernels, add_expanded(): pl.pallas_call(functools.partial(expand_kernel, counts, rank), grid_spec=...  7.09 us
    ppermute x2, starting transfers between devices, local_line(): lax.ppermute(low, 'tensor', [(i, i ^ bit) for i in range(4)])  5.06 us
  transfers between devices with their start and end apart: 17, of which 5 were waited for; matrix products, arithmetic and copies ran while one was open for 4% of the time, Pallas kernels for 27%

profile of v2, /device:TPU:0, one launch (start us, length us, event | category | flops | bytes accessed | tf_op | source)
XLA Modules:
  0.0 136.0 jit_solution(854742208965342130)
XLA Ops:
  0.5 2.6 %collective-permute-start = (bf16[384,2048]{1,0:T(8,128)(2,1)}, bf16[384,2048]{1,0:T(8,128)(2,1)}, u32[]{:S(2)}, u32[]{:S(2)}) collective-permute-start(bf16[384,2048]{1,0:T(8,128)(2,1)} %refs_1_.9), channel_id=1, source_target_pairs={{0,4},{4,0},{8,12},{12,8},{1,5},{5,1},{9,13},{13,9},{2,6},{6,2},{1... | collective-permute-start | bytes 4718600 | tf_op jit(solution)/shard_map/ppermute | solution.py:186
  3.1 1.8 %collective-permute-start.1 = (bf16[384,2048]{1,0:T(8,128)(2,1)}, bf16[384,2048]{1,0:T(8,128)(2,1)}, u32[]{:S(2)}, u32[]{:S(2)}) collective-permute-start(bf16[384,2048]{1,0:T(8,128)(2,1)} %refs_1_.9), channel_id=1, source_target_pairs={{4,8},{8,4},{5,9},{9,5},{6,10},{10,6},{7,11},{11,7},{20,24},{24,20... | collective-permute-start | bytes 4718600 | tf_op jit(solution)/shard_map/ppermute | solution.py:187
  4.9 2.3 %constant_dynamic-slice_fusion.1 = bf16[256,2048]{1,0:T(8,128)(2,1)} fusion(bf16[512,2048]{1,0:T(8,128)(2,1)} %bitcast.12, s32[]{:T(128)S(6)} %select_n.18), kind=kLoop, calls=%fused_computation.4 | loop fusion | bytes 2097156 | tf_op jit(solution)/shard_map/dynamic_slice | solution.py:138
  7.2 1.5 %collective-permute-start.2 = (bf16[256,2048]{1,0:T(8,128)(2,1)}, bf16[256,2048]{1,0:T(8,128)(2,1)}, u32[]{:S(2)}, u32[]{:S(2)}) collective-permute-start(bf16[256,2048]{1,0:T(8,128)(2,1)} %constant_dynamic-slice_fusion.1), channel_id=1, source_target_pairs={{0,2},{2,0},{1,3},{3,1},{4,6},{6,4},{5,7},{7,5},{8,10},{10,8},{9,1... | collective-permute-start | bytes 3145736 | tf_op jit(solution)/shard_map/ppermute | solution.py:191
  9.0 6.4 %shard_map.55.refs_2_ = f32[384,2048]{1,0:T(8,128)S(1)} custom-call(s32[1]{0:T(128)} %bitcast.3.row_block, bf16[384,2048]{1,0:T(8,128)(2,1)S(1)} %copy-done, bf16[8192,2048]{1,0:T(8,128)(2,1)} %refs_2_.3), custom_call_target="tpu_custom_call" | custom-call | flops 644245120 | bytes 2936012 | tf_op jit(solution)/shard_map/pallas_call | solution.py:66
  15.4 1.6 %copy-done.3 = f32[384,2048]{1,0:T(8,128)} copy-done((f32[384,2048]{1,0:T(8,128)}, f32[384,2048]{1,0:T(8,128)S(1)}, u32[]{:S(2)}) %copy-start.3) | copy-done | bytes 3145752
  17.0 1.6 %copy-done.5 = bf16[8,64,2048]{2,1,0:T(8,128)(2,1)S(1)} copy-done((bf16[8,64,2048]{2,1,0:T(8,128)(2,1)S(1)}, bf16[8,64,2048]{2,1,0:T(8,128)(2,1)}, u32[]{:S(2)}) %copy-start.5) | copy-done | bytes 2097176
  18.6 2.1 %shard_map.56 = (f32[384,64]{1,0:T(8,128)S(1)}, f32[384,64]{1,0:T(8,128)S(1)}) custom-call(s32[1]{0:T(128)} %bitcast.4.first, bf16[512,2048]{1,0:T(8,128)(2,1)S(1)} %bitcast.13, bf16[384,2048]{1,0:T(8,128)(2,1)S(1)} %copy-done, bf16[384,2048]{1,0:T(8,128)(2,1)S(1)} %collective-permute-done.3.refs_2_, s32[384,1]{1,0:T(8,128)S(1)} %copy.7.refs_3_.owner_ref, ...), custom_call_target="tpu_custom_call" | custom-call | flops 322122560 | bytes 1048576 | tf_op jit(solution)/shard_map/pallas_call | solution.py:159
  21.4 0.7 copy-done.12
  22.1 10.6 %collective-permute-done.2.refs_0_ = bf16[256,2048]{1,0:T(8,128)(2,1)} collective-permute-done((bf16[256,2048]{1,0:T(8,128)(2,1)}, bf16[256,2048]{1,0:T(8,128)(2,1)}, u32[]{:S(2)}, u32[]{:S(2)}) %collective-permute-start.2) | collective-permute-done | bytes 1048608 | tf_op jit(solution)/shard_map/ppermute | solution.py:191
  32.8 1.5 %collective-permute-start.7 = (bf16[256,2048]{1,0:T(8,128)(2,1)}, bf16[256,2048]{1,0:T(8,128)(2,1)}, u32[]{:S(2)}, u32[]{:S(2)}) collective-permute-start(bf16[256,2048]{1,0:T(8,128)(2,1)} %collective-permute-done.2.refs_0_), channel_id=1, source_target_pairs={{0,16},{16,0},{1,17},{17,1},{2,18},{18,2},{3,19},{19,3},{4,20},{20... | collective-permute-start | bytes 3145736 | tf_op jit(solution)/shard_map/ppermute | solution.py:195
  34.3 2.3 %constant_dynamic-slice_fusion = bf16[256,2048]{1,0:T(8,128)(2,1)} fusion(bf16[512,2048]{1,0:T(8,128)(2,1)} %bitcast.11.rest_0_, s32[]{:T(128)S(6)} %select_n.18), kind=kLoop, calls=%fused_computation.3 | loop fusion | bytes 2097156 | tf_op jit(solution)/shard_map/dynamic_slice | solution.py:138
  36.6 1.5 %collective-permute-start.12 = (bf16[256,2048]{1,0:T(8,128)(2,1)}, bf16[256,2048]{1,0:T(8,128)(2,1)}, u32[]{:S(2)}, u32[]{:S(2)}) collective-permute-start(bf16[256,2048]{1,0:T(8,128)(2,1)} %constant_dynamic-slice_fusion), channel_id=1, source_target_pairs={{0,2},{2,0},{1,3},{3,1},{4,6},{6,4},{5,7},{7,5},{8,10},{10,8},{9,1... | collective-permute-start | bytes 3145736 | tf_op jit(solution)/shard_map/ppermute | solution.py:192
  38.1 0.9 copy-done.11
  39.0 0.9 copy-done.13
  39.9 3.3 %shard_map.57 = (f32[384,64]{1,0:T(8,128)S(1)}, f32[384,64]{1,0:T(8,128)S(1)}) custom-call(s32[1]{0:T(128)} %bitcast.1.first, bf16[256,2048]{1,0:T(8,128)(2,1)} %collective-permute-done.2.refs_0_, bf16[384,2048]{1,0:T(8,128)(2,1)S(1)} %copy-done, bf16[384,2048]{1,0:T(8,128)(2,1)S(1)} %collective-permute-done.3.refs_2_, s32[384,1]{1,0:T(8,128)S(1)} %copy.7.refs_3_.owner_ref, ...), custom_call_target="tpu_custom_call" | custom-call | flops 161061280 | bytes 524288 | tf_op jit(solution)/shard_map/pallas_call | solution.py:159
  43.9 0.7 copy-done.8
  44.6 1.9 %collective-permute-start.5 = (bf16[384,2048]{1,0:T(8,128)(2,1)}, bf16[384,2048]{1,0:T(8,128)(2,1)}, u32[]{:S(2)}, u32[]{:S(2)}) collective-permute-start(bf16[384,2048]{1,0:T(8,128)(2,1)} %collective-permute-done.refs_0_), channel_id=1, source_target_pairs={{4,8},{8,4},{5,9},{9,5},{6,10},{10,6},{7,11},{11,7},{20,24},{24,20... | collective-permute-start | bytes 4718600 | tf_op jit(solution)/shard_map/ppermute | solution.py:198
  46.4 1.3 collective-permute-start.6
  47.8 1.9 %copy-done.4 = f32[384,2048]{1,0:T(8,128)S(1)} copy-done((f32[384,2048]{1,0:T(8,128)S(1)}, f32[384,2048]{1,0:T(8,128)}, u32[]{:S(2)}) %copy-start.4) | copy-done | bytes 3145752
  49.6 7.0 %shard_map.58.refs_3_ = f32[384,2048]{1,0:T(8,128)S(1)} custom-call(s32[1]{0:T(128)} %bitcast.6.row_block, bf16[384,2048]{1,0:T(8,128)(2,1)} %collective-permute-done.refs_0_, bf16[8192,2048]{1,0:T(8,128)(2,1)} %refs_2_.3, f32[384,2048]{1,0:T(8,128)S(1)} %copy-done.4), custom_call_target="tpu_custom_call" | custom-call | flops 644245120 | bytes 2936012 | tf_op jit(solution)/shard_map/pallas_call | solution.py:66
  56.7 1.6 %copy-done.1 = f32[384,2048]{1,0:T(8,128)} copy-done((f32[384,2048]{1,0:T(8,128)}, f32[384,2048]{1,0:T(8,128)S(1)}, u32[]{:S(2)}) %copy-start.1) | copy-done | bytes 3145752
  58.3 3.3 %shard_map.59 = (f32[384,64]{1,0:T(8,128)S(1)}, f32[384,64]{1,0:T(8,128)S(1)}) custom-call(s32[1]{0:T(128)} %bitcast.5.first, bf16[256,2048]{1,0:T(8,128)(2,1)} %collective-permute-done.7.refs_0_, bf16[384,2048]{1,0:T(8,128)(2,1)S(1)} %copy-done, bf16[384,2048]{1,0:T(8,128)(2,1)S(1)} %collective-permute-done.3.refs_2_, s32[384,1]{1,0:T(8,128)S(1)} %copy.7.refs_3_.owner_ref, ...), custom_call_target="tpu_custom_call" | custom-call | flops 161061280 | bytes 524288 | tf_op jit(solution)/shard_map/pallas_call | solution.py:159
  63.0 4.6 %collective-permute-start.9 = (bf16[384,64]{1,0:T(8,128)(2,1)S(1)}, bf16[384,64]{1,0:T(8,128)(2,1)S(1)}, u32[]{:S(2)}, u32[]{:S(2)}) collective-permute-start(bf16[384,64]{1,0:T(8,128)(2,1)S(1)} %add_convert_fusion.2), channel_id=1, source_target_pairs={{0,4},{4,0},{8,12},{12,8},{1,5},{5,1},{9,13},{13,9},{2,6},{6,2},{1... | collective-permute-start | bytes 147464 | tf_op jit(solution)/shard_map/ppermute | solution.py:206
  67.6 18.8 %collective-permute-done.9 = bf16[384,64]{1,0:T(8,128)(2,1)S(1)} collective-permute-done((bf16[384,64]{1,0:T(8,128)(2,1)S(1)}, bf16[384,64]{1,0:T(8,128)(2,1)S(1)}, u32[]{:S(2)}, u32[]{:S(2)}) %collective-permute-start.9) | collective-permute-done | bytes 49184 | tf_op jit(solution)/shard_map/ppermute | solution.py:206
  86.9 5.6 %collective-permute-done.10 = bf16[384,64]{1,0:T(8,128)(2,1)S(1)} collective-permute-done((bf16[384,64]{1,0:T(8,128)(2,1)S(1)}, bf16[384,64]{1,0:T(8,128)(2,1)S(1)}, u32[]{:S(2)}, u32[]{:S(2)}) %collective-permute-start.10) | collective-permute-done | bytes 49184 | tf_op jit(solution)/shard_map/ppermute | solution.py:206
  92.5 1.3 collective-permute-start.11
  94.5 1.9 %copy-done.2 = f32[384,2048]{1,0:T(8,128)S(1)} copy-done((f32[384,2048]{1,0:T(8,128)S(1)}, f32[384,2048]{1,0:T(8,128)}, u32[]{:S(2)}) %copy-start.2) | copy-done | bytes 3145752
  96.4 7.5 %shard_map.60.acc_ref = f32[384,2048]{1,0:T(8,128)S(1)} custom-call(s32[1]{0:T(128)} %bitcast.10.row_block, bf16[384,2048]{1,0:T(8,128)(2,1)} %collective-permute-done.1.refs_0_, bf16[384,2048]{1,0:T(8,128)(2,1)} %collective-permute-done.6.refs_1_, bf16[8192,2048]{1,0:T(8,128)(2,1)} %refs_2_.3, f32[384,2048]{1,0:T(8,128)S(1)} %copy-done.2), custom_call_target="tpu_custom_call" | custom-call | flops 644245120 | bytes 2936012 | tf_op jit(solution)/shard_map/pallas_call | solution.py:66
  103.9 7.1 %shard_map.61.refs_3_ = f32[384,2048]{1,0:T(8,128)S(1)} custom-call(s32[6]{0:T(128)S(1)} %stack.18.firsts, bf16[384,64]{1,0:T(8,128)(2,1)S(1)} %add_convert_fusion.low_ref, s32[384,1]{1,0:T(8,128)S(1)} %copy.7.refs_3_.owner_ref, f32[384,2048]{1,0:T(8,128)S(1)} %shard_map.60.acc_ref, bf16[512,2048]{1,0:T(8,128)(2,1)} %bitcast.11.rest_0_, ...), custom_call_target="tpu_custom_call" | custom-call | flops 644245120 | bytes 2936012 | tf_op jit(solution)/shard_map/pallas_call | solution.py:111
  110.9 16.8 %collective-permute-done.11.refs_1_ = bf16[384,2048]{1,0:T(8,128)(2,1)} collective-permute-done((bf16[384,2048]{1,0:T(8,128)(2,1)}, bf16[384,2048]{1,0:T(8,128)(2,1)}, u32[]{:S(2)}, u32[]{:S(2)}) %collective-permute-start.11) | collective-permute-done | bytes 1572896 | tf_op jit(solution)/shard_map/ppermute | solution.py:211
  127.8 8.2 %shard_map.62 = bf16[384,2048]{1,0:T(8,128)(2,1)} custom-call(s32[1]{0:T(128)} %bitcast.row_block, bf16[384,2048]{1,0:T(8,128)(2,1)} %collective-permute-done.5.refs_0_, bf16[384,2048]{1,0:T(8,128)(2,1)} %collective-permute-done.11.refs_1_, bf16[8192,2048]{1,0:T(8,128)(2,1)} %refs_2_.3, f32[384,2048]{1,0:T(8,128)S(1)} %shard_map.61.refs_3_), custom_call_target="tpu_custom_call" | custom-call | flops 644245120 | bytes 2936012 | tf_op jit(solution)/shard_map/pallas_call | solution.py:66
  (48 shorter events, 4.6 us)
Async XLA Ops:
  0.0 8.9 %copy-start = (bf16[384,2048]{1,0:T(8,128)(2,1)S(1)}, bf16[384,2048]{1,0:T(8,128)(2,1)}, u32[]{:S(2)}) copy-start(bf16[384,2048]{1,0:T(8,128)(2,1)} %refs_1_.9) | copy-start | bytes 4718596
  0.0 8.7 %copy-start.14 = (s32[384,1]{0,1:T(1,128)S(1)}, s32[384,1]{0,1:T(1,128)}, u32[]{:S(2)}) copy-start(s32[384,1]{0,1:T(1,128)} %param.9) | copy-start | bytes 4612
  0.0 17.0 %collective-permute-start.3 = (bf16[384,2048]{1,0:T(8,128)(2,1)}, bf16[384,2048]{1,0:T(8,128)(2,1)S(1)}, u32[]{:S(2)}, u32[]{:S(2)}) collective-permute-start(bf16[384,2048]{1,0:T(8,128)(2,1)} %refs_1_.9), channel_id=1, source_target_pairs={{0,1},{1,0},{2,3},{3,2},{4,5},{5,4},{6,7},{7,6},{8,9},{9,8},{10,11... | collective-permute-start | bytes 4718600 | tf_op jit(solution)/shard_map/ppermute | solution.py:189
  0.5 44.1 %collective-permute-start = (bf16[384,2048]{1,0:T(8,128)(2,1)}, bf16[384,2048]{1,0:T(8,128)(2,1)}, u32[]{:S(2)}, u32[]{:S(2)}) collective-permute-start(bf16[384,2048]{1,0:T(8,128)(2,1)} %refs_1_.9), channel_id=1, source_target_pairs={{0,4},{4,0},{8,12},{12,8},{1,5},{5,1},{9,13},{13,9},{2,6},{6,2},{1... | collective-permute-start | bytes 4718600 | tf_op jit(solution)/shard_map/ppermute | solution.py:186
  3.1 41.5 %collective-permute-start.1 = (bf16[384,2048]{1,0:T(8,128)(2,1)}, bf16[384,2048]{1,0:T(8,128)(2,1)}, u32[]{:S(2)}, u32[]{:S(2)}) collective-permute-start(bf16[384,2048]{1,0:T(8,128)(2,1)} %refs_1_.9), channel_id=1, source_target_pairs={{4,8},{8,4},{5,9},{9,5},{6,10},{10,6},{7,11},{11,7},{20,24},{24,20... | collective-permute-start | bytes 4718600 | tf_op jit(solution)/shard_map/ppermute | solution.py:187
  7.2 25.5 %collective-permute-start.2 = (bf16[256,2048]{1,0:T(8,128)(2,1)}, bf16[256,2048]{1,0:T(8,128)(2,1)}, u32[]{:S(2)}, u32[]{:S(2)}) collective-permute-start(bf16[256,2048]{1,0:T(8,128)(2,1)} %constant_dynamic-slice_fusion.1), channel_id=1, source_target_pairs={{0,2},{2,0},{1,3},{3,1},{4,6},{6,4},{5,7},{7,5},{8,10},{10,8},{9,1... | collective-permute-start | bytes 3145736 | tf_op jit(solution)/shard_map/ppermute | solution.py:191
  8.9 8.2 %collective-permute-start.4 = (s32[384,1]{1,0:T(8,128)S(1)}, s32[384,1]{1,0:T(8,128)S(1)}, u32[]{:S(2)}, u32[]{:S(2)}) collective-permute-start(s32[384,1]{1,0:T(8,128)S(1)} %copy.7.refs_3_.owner_ref), channel_id=1, source_target_pairs={{0,1},{1,0},{2,3},{3,2},{4,5},{5,4},{6,7},{7,6},{8,9},{9,8},{10,11... | collective-permute-start | bytes 4616 | tf_op jit(solution)/shard_map/ppermute | solution.py:190
  15.4 1.6 %copy-start.3 = (f32[384,2048]{1,0:T(8,128)}, f32[384,2048]{1,0:T(8,128)S(1)}, u32[]{:S(2)}) copy-start(f32[384,2048]{1,0:T(8,128)S(1)} %shard_map.55.refs_2_) | copy-start | bytes 9437188
  17.0 1.6 %copy-start.5 = (bf16[8,64,2048]{2,1,0:T(8,128)(2,1)S(1)}, bf16[8,64,2048]{2,1,0:T(8,128)(2,1)}, u32[]{:S(2)}) copy-start(bf16[8,64,2048]{2,1,0:T(8,128)(2,1)} %param.7) | copy-start | bytes 6291460
  20.8 0.7 copy-start.10
  21.4 0.7 copy-start.12
  32.8 25.5 %collective-permute-start.7 = (bf16[256,2048]{1,0:T(8,128)(2,1)}, bf16[256,2048]{1,0:T(8,128)(2,1)}, u32[]{:S(2)}, u32[]{:S(2)}) collective-permute-start(bf16[256,2048]{1,0:T(8,128)(2,1)} %collective-permute-done.2.refs_0_), channel_id=1, source_target_pairs={{0,16},{16,0},{1,17},{17,1},{2,18},{18,2},{3,19},{19,3},{4,20},{20... | collective-permute-start | bytes 3145736 | tf_op jit(solution)/shard_map/ppermute | solution.py:195
  36.6 25.6 %collective-permute-start.12 = (bf16[256,2048]{1,0:T(8,128)(2,1)}, bf16[256,2048]{1,0:T(8,128)(2,1)}, u32[]{:S(2)}, u32[]{:S(2)}) collective-permute-start(bf16[256,2048]{1,0:T(8,128)(2,1)} %constant_dynamic-slice_fusion), channel_id=1, source_target_pairs={{0,2},{2,0},{1,3},{3,1},{4,6},{6,4},{5,7},{7,5},{8,10},{10,8},{9,1... | collective-permute-start | bytes 3145736 | tf_op jit(solution)/shard_map/ppermute | solution.py:192
  38.1 0.9 copy-start.11
  39.0 0.9 copy-start.13
  43.2 0.7 copy-start.6
  43.9 0.7 copy-start.8
  44.6 47.9 %collective-permute-start.5 = (bf16[384,2048]{1,0:T(8,128)(2,1)}, bf16[384,2048]{1,0:T(8,128)(2,1)}, u32[]{:S(2)}, u32[]{:S(2)}) collective-permute-start(bf16[384,2048]{1,0:T(8,128)(2,1)} %collective-permute-done.refs_0_), channel_id=1, source_target_pairs={{4,8},{8,4},{5,9},{9,5},{6,10},{10,6},{7,11},{11,7},{20,24},{24,20... | collective-permute-start | bytes 4718600 | tf_op jit(solution)/shard_map/ppermute | solution.py:198
  46.4 46.0 %collective-permute-start.6 = (bf16[384,2048]{1,0:T(8,128)(2,1)}, bf16[384,2048]{1,0:T(8,128)(2,1)}, u32[]{:S(2)}, u32[]{:S(2)}) collective-permute-start(bf16[384,2048]{1,0:T(8,128)(2,1)} %collective-permute-done.1.refs_0_), channel_id=1, source_target_pairs={{4,0},{8,12},{5,1},{9,13},{6,2},{10,14},{7,3},{11,15},{20,16},{24,... | collective-permute-start | bytes 4718600 | tf_op jit(solution)/shard_map/ppermute | solution.py:199
  47.7 1.9 %copy-start.4 = (f32[384,2048]{1,0:T(8,128)S(1)}, f32[384,2048]{1,0:T(8,128)}, u32[]{:S(2)}) copy-start(f32[384,2048]{1,0:T(8,128)} %copy-done.3) | copy-start | bytes 9437188
  49.6 8.7 %copy-start.7 = (f32[384,64]{1,0:T(8,128)S(1)}, f32[384,64]{1,0:T(8,128)}, u32[]{:S(2)}) copy-start(f32[384,64]{1,0:T(8,128)} %copy-done.6) | copy-start | bytes 294916
  49.6 8.7 %copy-start.9 = (f32[384,64]{1,0:T(8,128)S(1)}, f32[384,64]{1,0:T(8,128)}, u32[]{:S(2)}) copy-start(f32[384,64]{1,0:T(8,128)} %copy-done.8) | copy-start | bytes 294916
  56.7 1.6 %copy-start.1 = (f32[384,2048]{1,0:T(8,128)}, f32[384,2048]{1,0:T(8,128)S(1)}, u32[]{:S(2)}) copy-start(f32[384,2048]{1,0:T(8,128)S(1)} %shard_map.58.refs_3_) | copy-start | bytes 9437188
  61.6 1.4 %collective-permute-start.8 = (bf16[384,64]{1,0:T(8,128)(2,1)S(1)}, bf16[384,64]{1,0:T(8,128)(2,1)S(1)}, u32[]{:S(2)}, u32[]{:S(2)}) collective-permute-start(bf16[384,64]{1,0:T(8,128)(2,1)S(1)} %convert_element_type.27), channel_id=1, source_target_pairs={{0,1},{1,0},{2,3},{3,2},{4,5},{5,4},{6,7},{7,6},{8,9},{9,8},{10,11... | collective-permute-start | bytes 147464 | tf_op jit(solution)/shard_map/ppermute | solution.py:203
  61.7 42.2 %collective-permute-start.14 = (bf16[512,2048]{1,0:T(8,128)(2,1)}, bf16[512,2048]{1,0:T(8,128)(2,1)S(1)}, u32[]{:S(2)}, u32[]{:S(2)}) collective-permute-start(bf16[512,2048]{1,0:T(8,128)(2,1)} %bitcast.11.rest_0_), channel_id=1, source_target_pairs={{0,1},{1,0},{2,3},{3,2},{4,5},{5,4},{6,7},{7,6},{8,9},{9,8},{10,11... | collective-permute-start | bytes 6291464 | tf_op jit(solution)/shard_map/ppermute | solution.py:215
  62.2 31.7 %collective-permute-start.13 = (bf16[256,2048]{1,0:T(8,128)(2,1)}, bf16[256,2048]{1,0:T(8,128)(2,1)S(1)}, u32[]{:S(2)}, u32[]{:S(2)}) collective-permute-start(bf16[256,2048]{1,0:T(8,128)(2,1)} %collective-permute-done.12.rest_1_), channel_id=1, source_target_pairs={{0,16},{16,0},{1,17},{17,1},{2,18},{18,2},{3,19},{19,3},{4,20},{20... | collective-permute-start | bytes 3145736 | tf_op jit(solution)/shard_map/ppermute | solution.py:213
  63.0 23.4 %collective-permute-start.9 = (bf16[384,64]{1,0:T(8,128)(2,1)S(1)}, bf16[384,64]{1,0:T(8,128)(2,1)S(1)}, u32[]{:S(2)}, u32[]{:S(2)}) collective-permute-start(bf16[384,64]{1,0:T(8,128)(2,1)S(1)} %add_convert_fusion.2), channel_id=1, source_target_pairs={{0,4},{4,0},{8,12},{12,8},{1,5},{5,1},{9,13},{13,9},{2,6},{6,2},{1... | collective-permute-start | bytes 147464 | tf_op jit(solution)/shard_map/ppermute | solution.py:206
  86.4 6.0 %collective-permute-start.10 = (bf16[384,64]{1,0:T(8,128)(2,1)S(1)}, bf16[384,64]{1,0:T(8,128)(2,1)S(1)}, u32[]{:S(2)}, u32[]{:S(2)}) collective-permute-start(bf16[384,64]{1,0:T(8,128)(2,1)S(1)} %add_convert_fusion.1), channel_id=1, source_target_pairs={{0,8},{4,12},{8,0},{12,4},{1,9},{5,13},{9,1},{13,5},{2,10},{6,14},... | collective-permute-start | bytes 147464 | tf_op jit(solution)/shard_map/ppermute | solution.py:206
  92.5 35.3 %collective-permute-start.11 = (bf16[384,2048]{1,0:T(8,128)(2,1)}, bf16[384,2048]{1,0:T(8,128)(2,1)}, u32[]{:S(2)}, u32[]{:S(2)}) collective-permute-start(bf16[384,2048]{1,0:T(8,128)(2,1)} %collective-permute-done.5.refs_0_), channel_id=1, source_target_pairs={{4,0},{8,12},{5,1},{9,13},{6,2},{10,14},{7,3},{11,15},{20,16},{24,... | collective-permute-start | bytes 4718600 | tf_op jit(solution)/shard_map/ppermute | solution.py:211
  93.8 10.0 %collective-permute-start.15 = (bf16[256,2048]{1,0:T(8,128)(2,1)}, bf16[256,2048]{1,0:T(8,128)(2,1)}, u32[]{:S(2)}, u32[]{:S(2)}) collective-permute-start(bf16[256,2048]{1,0:T(8,128)(2,1)} %collective-permute-done.12.rest_1_), channel_id=1, source_target_pairs={{0,1},{1,0},{2,3},{3,2},{4,5},{5,4},{6,7},{7,6},{8,9},{9,8},{10,11... | collective-permute-start | bytes 3145736 | tf_op jit(solution)/shard_map/ppermute | solution.py:215
  93.9 10.0 %collective-permute-start.16 = (bf16[256,2048]{1,0:T(8,128)(2,1)S(1)}, bf16[256,2048]{1,0:T(8,128)(2,1)}, u32[]{:S(2)}, u32[]{:S(2)}) collective-permute-start(bf16[256,2048]{1,0:T(8,128)(2,1)S(1)} %collective-permute-done.13.rest_2_), channel_id=1, source_target_pairs={{0,1},{1,0},{2,3},{3,2},{4,5},{5,4},{6,7},{7,6},{8,9},{9,8},{10,11... | collective-permute-start | bytes 3145736 | tf_op jit(solution)/shard_map/ppermute | solution.py:215
  94.5 1.9 %copy-start.2 = (f32[384,2048]{1,0:T(8,128)S(1)}, f32[384,2048]{1,0:T(8,128)}, u32[]{:S(2)}) copy-start(f32[384,2048]{1,0:T(8,128)} %copy-done.1) | copy-start | bytes 9437188

commit v3 on v2

--- a/solution.py
+++ b/solution.py
@@ -9,6 +9,7 @@
 
 adapter_scale = 0.5
 TILE = 512
+PIECES = 4
 TINY = 0.2
 SHRINK = 0.2
 FIRST = 0.2
@@ -72,6 +73,59 @@
         compiler_params=PARAMS,
         cost_estimate=cost(rows, depth, cols, share),
     )(*args)
+
+
+def last_kernel(inner, here, there, weight_ref, acc_ref, out, x_ref, tiles_ref, came, went):
+    depth, cols = weight_ref.shape
+    step = depth // PIECES
+    pieces = [pl.ds(i * step, step) for i in range(PIECES)]
+    wide = cols // PIECES
+    spans = [pl.ds(i * wide, wide) for i in range(PIECES)]
+
+    def arriving(source, i):
+        return pltpu.make_async_copy(source.at[:, pieces[i]], x_ref.at[:, pieces[i]], came.at[i])
+
+    for source, chosen in ((here, inner[0] == 1), (there, inner[0] == 0)):
+
+        @pl.when(chosen)
+        def _(source=source):
+            for i in range(PIECES):
+                arriving(source, i).start()
+
+    leaving = []
+    for n, span in enumerate(spans):
+        total = acc_ref[:, span]
+        for i, piece in enumerate(pieces):
+            if n == 0:
+                arriving(there, i).wait()
+            total += jnp.dot(
+                x_ref[:, piece], weight_ref[piece, span], preferred_element_type=jnp.float32
+            )
+        tiles_ref[:, span] = total.astype(tiles_ref.dtype)
+        leaving.append(pltpu.make_async_copy(tiles_ref.at[:, span], out.at[:, span], went.at[n]))
+        leaving[-1].start()
+    for copy in leaving:
+        copy.wait()
+
+
+def add_last(acc, inner, here, there, weight):
+    rows, depth = here.shape
+    cols = weight.shape[1]
+    anywhere, resident = pl.BlockSpec(memory_space=pl.ANY), pl.BlockSpec(memory_space=pltpu.VMEM)
+    return pl.pallas_call(
+        last_kernel,
+        in_specs=[pl.BlockSpec(memory_space=pltpu.SMEM), anywhere, anywhere, resident, resident],
+        out_specs=anywhere,
+        out_shape=jax.ShapeDtypeStruct((rows, cols), jnp.bfloat16),
+        scratch_shapes=[
+            pltpu.VMEM((rows, depth), jnp.bfloat16),
+            pltpu.VMEM((rows, cols), jnp.bfloat16),
+            pltpu.SemaphoreType.DMA((PIECES,)),
+            pltpu.SemaphoreType.DMA((PIECES,)),
+        ],
+        compiler_params=pltpu.CompilerParams(vmem_limit_bytes=30 * 2**20),
+        cost_estimate=cost(rows, depth, cols, TINY),
+    )(inner.astype(jnp.int32).reshape(1), here, there, weight, acc)
 
 
 def expand_kernel(counts, rank, firsts, low_ref, owner_ref, acc_ref, *rest):
@@ -189,36 +243,39 @@
     xs = (requests, lax.ppermute(requests, "adapter", BESIDE))
     both = (owners, lax.ppermute(owners, "adapter", BESIDE))
     down_mine = lax.ppermute(half_of(down, replica), "adapter", ACROSS)
-    up_mine = lax.ppermute(half_of(up, replica), "adapter", ACROSS)
+    up_half, up_near = half_of(up, replica), lax.ppermute(up, "adapter", BESIDE)
     lows = add_shrunk((), down, halves[0], xs, both, rank)
-    down_mine, acc, lows = lax.optimization_barrier((down_mine, acc, lows))
+    down_mine, acc, lows, up_half, up_near = lax.optimization_barrier(
+        (down_mine, acc, lows, up_half, up_near)
+    )
+    up_mine = lax.ppermute(up_half, "adapter", ACROSS)
     down_other = lax.ppermute(down_mine, "replica", SWAP)
+    a1, down_mine = lax.optimization_barrier((a1, down_mine))
     lows = add_shrunk(lows, down_mine, halves[1], xs, both, rank)
-    a1, m1, lows = lax.optimization_barrier((a1, m1, lows))
     m2 = lax.ppermute(a1, "tensor", middle)
+    m1, a1 = lax.optimization_barrier((m1, a1))
     e2 = lax.ppermute(m1, "tensor", outward)
     acc = add_block(acc, [[a1]], query_weight, z ^ 1)
     lows, acc = lax.optimization_barrier((lows, acc))
     lows = add_shrunk(lows, down_other, halves[2], xs, both, rank)
     low = lows[0] + lax.ppermute(lows[1].astype(jnp.bfloat16), "adapter", BESIDE).astype(jnp.float32)
-    for bit in (1, 2):
-        low = low.astype(jnp.bfloat16)
-        low = low.astype(jnp.float32) + lax.ppermute(
-            low, "tensor", [(i, i ^ bit) for i in range(4)]
-        ).astype(jnp.float32)
-    low = low.astype(jnp.bfloat16)
+    shares = jnp.broadcast_to(low.astype(jnp.bfloat16)[None], (4, *low.shape))
+    shares = lax.all_to_all(shares, "tensor", 0, 0)
+    low = jnp.sum(shares.astype(jnp.float32), axis=0).astype(jnp.bfloat16)
     m2, e2, low = lax.optimization_barrier((m2, e2, low))
     e3 = lax.ppermute(m2, "tensor", outward)
 
     up_other = lax.ppermute(up_mine, "replica", SWAP)
     up_other, _ = lax.optimization_barrier((up_other, m2))
-    near = [lax.ppermute(piece, "adapter", BESIDE) for piece in (up, up_mine, up_other)]
+    near = [up_near, *[lax.ppermute(piece, "adapter", BESIDE) for piece in (up_mine, up_other)]]
     across = resident - 2 * (me % 2) * resident
     ups = list(zip((up, up_mine, up_other), halves)) + list(zip(near, [h + across for h in halves]))
 
     acc = add_block(acc, [[m1, e2]], query_weight, second)
+    weight = lax.dynamic_slice_in_dim(query_weight, third * features, features, 0)
+    acc, weight = lax.optimization_barrier((acc, weight))
     acc = add_expanded(acc, low, owners, ups)
-    return add_block(acc, [[m2, e3]], query_weight, third, jnp.bfloat16)
+    return add_last(acc, inner, m2, e3, weight)
 
 
 def local_any(requests, query_weight, adapter_down_factor, adapter_up_factor, owners):

time: 137 us -> 130 us (0.949)
  waiting for transfers between devices: 51.9 us -> 26 us
  blocking collectives: 0 us -> 21.1 us
  starting transfers between devices: 20.8 us -> 16.6 us
  local copies, waits for them, and re-layouts: 18 us -> 22 us
  Pallas kernels: 44.9 us -> 42.8 us
    all_to_all x0 -> x1, blocking collectives: none -> 21.1 us  [local_line(): shares = lax.all_to_all(shares, 'tensor', 0, 0)]
    ppermute x3 -> x2, waiting for transfers between devices: 24.4 us -> 3.96 us  [the longest x1 3.96 us: local_line(): up_mine = lax.ppermute(up_half, 'adapter', ACROSS)]
    dynamic_slice x0 -> x1, local copies, waits for them, and re-layouts: none -> 8.48 us  [local_line(): lax.dynamic_slice_in_dim(query_weight, third * features, features, 0)]
    pallas_call x4 -> x3, Pallas kernels: 29.1 us -> 21 us  [add_block(): pl.pallas_call(functools.partial(block_kernel, tuple((len(group) for grou...]
    ppermute x1, waiting for transfers between devices: 16.8 us -> 9.06 us  [local_line(): e3 = lax.ppermute(m2, 'tensor', outward)]
    pallas_call x0 -> x1, Pallas kernels: none -> 5.39 us  [add_last(): pl.pallas_call(last_kernel, in_specs=[pl.BlockSpec(memory_space=pltpu.SME...]
    ppermute x3 -> x2, starting transfers between devices: 6.55 us -> 1.94 us  [the longest x1 1.49 us: local_line(): up_mine = lax.ppermute(up_half, 'adapter', ACROSS)]
    unnamed x31 -> x27, local copies, waits for them, and re-layouts: 13.3 us -> 9.77 us
  transfers between devices with their start and end apart: 17 -> 15, of which waited for: 5 -> 5; matrix products, arithmetic and copies ran while one was open for 4% -> 10% of each run, Pallas kernels for 27% -> 29%
where the time goes in v3:
time: 130 us; the launch traced here: 129 us
  Pallas kernels  42.8 us (33%)
  waiting for transfers between devices  26 us (20%)
  local copies, waits for them, and re-layouts  22 us (17%)
  blocking collectives  21.1 us (16%)
  starting transfers between devices  16.6 us (13%)
    all_to_all x1, blocking collectives, local_line(): shares = lax.all_to_all(shares, 'tensor', 0, 0)  21.1 us
    pallas_call x3, Pallas kernels, add_block(): pl.pallas_call(functools.partial(block_kernel, tuple((len(group) for grou...  21 us
    ppermute x1, waiting for transfers between devices, local_line(): down_mine = lax.ppermute(half_of(down, replica), 'adapter', ACROSS)  10.7 us
    unnamed x27, local copies, waits for them, and re-layouts  9.77 us
    ppermute x1, waiting for transfers between devices, local_line(): e3 = lax.ppermute(m2, 'tensor', outward)  9.06 us
    pallas_call x3, Pallas kernels, add_shrunk(): pl.pallas_call(functools.partial(shrink_kernel, piece.shape[0] // rank, r...  8.82 us
    dynamic_slice x1, local copies, waits for them, and re-layouts, local_line(): lax.dynamic_slice_in_dim(query_weight, third * features, features, 0)  8.48 us
    pallas_call x1, Pallas kernels, add_expanded(): pl.pallas_call(functools.partial(expand_kernel, counts, rank), grid_spec=...  7.61 us
  transfers between devices with their start and end apart: 15, of which 5 were waited for; matrix products, arithmetic and copies ran while one was open for 10% of the time, Pallas kernels for 29%

profile of v3, /device:TPU:0, one launch (start us, length us, event | category | flops | bytes accessed | tf_op | source)
XLA Modules:
  0.0 129.1 jit_solution(2652881856577179939)
XLA Ops:
  0.5 3.0 %collective-permute-start = (bf16[384,2048]{1,0:T(8,128)(2,1)}, bf16[384,2048]{1,0:T(8,128)(2,1)}, u32[]{:S(2)}, u32[]{:S(2)}) collective-permute-start(bf16[384,2048]{1,0:T(8,128)(2,1)} %refs_1_.9), channel_id=1, source_target_pairs={{0,4},{4,0},{8,12},{12,8},{1,5},{5,1},{9,13},{13,9},{2,6},{6,2},{1... | collective-permute-start | bytes 4718600 | tf_op jit(solution)/shard_map/ppermute | solution.py:240
  3.5 1.8 %collective-permute-start.6 = (bf16[384,2048]{1,0:T(8,128)(2,1)}, bf16[384,2048]{1,0:T(8,128)(2,1)}, u32[]{:S(2)}, u32[]{:S(2)}) collective-permute-start(bf16[384,2048]{1,0:T(8,128)(2,1)} %refs_1_.9), channel_id=1, source_target_pairs={{4,8},{8,4},{5,9},{9,5},{6,10},{10,6},{7,11},{11,7},{20,24},{24,20... | collective-permute-start | bytes 4718600 | tf_op jit(solution)/shard_map/ppermute | solution.py:241
  6.2 2.3 %constant_dynamic-slice_fusion.2 = bf16[256,2048]{1,0:T(8,128)(2,1)} fusion(bf16[512,2048]{1,0:T(8,128)(2,1)} %bitcast.12, s32[]{:T(128)S(6)} %select_n.20), kind=kLoop, calls=%fused_computation.3 | loop fusion | bytes 2097156 | tf_op jit(solution)/shard_map/dynamic_slice | solution.py:192
  8.5 1.5 %collective-permute-start.1 = (bf16[256,2048]{1,0:T(8,128)(2,1)}, bf16[256,2048]{1,0:T(8,128)(2,1)}, u32[]{:S(2)}, u32[]{:S(2)}) collective-permute-start(bf16[256,2048]{1,0:T(8,128)(2,1)} %constant_dynamic-slice_fusion.2), channel_id=1, source_target_pairs={{0,2},{2,0},{1,3},{3,1},{4,6},{6,4},{5,7},{7,5},{8,10},{10,8},{9,1... | collective-permute-start | bytes 3145736 | tf_op jit(solution)/shard_map/ppermute | solution.py:245
  10.0 6.6 %shard_map.55.refs_2_ = f32[384,2048]{1,0:T(8,128)S(1)} custom-call(s32[1]{0:T(128)} %bitcast.2.row_block, bf16[384,2048]{1,0:T(8,128)(2,1)S(1)} %copy-done.1, bf16[8192,2048]{1,0:T(8,128)(2,1)} %refs_2_.1), custom_call_target="tpu_custom_call" | custom-call | flops 644245120 | bytes 2936012 | tf_op jit(solution)/shard_map/pallas_call | solution.py:67
  16.6 1.6 %copy-done.4 = f32[384,2048]{1,0:T(8,128)} copy-done((f32[384,2048]{1,0:T(8,128)}, f32[384,2048]{1,0:T(8,128)S(1)}, u32[]{:S(2)}) %copy-start.4) | copy-done | bytes 3145752
  18.2 1.1 constant_dynamic-slice_fusion.1
  19.4 0.8 copy-done.6
  20.2 2.2 %shard_map.56 = (f32[384,64]{1,0:T(8,128)S(1)}, f32[384,64]{1,0:T(8,128)S(1)}) custom-call(s32[1]{0:T(128)} %bitcast.3.first, bf16[512,2048]{1,0:T(8,128)(2,1)S(1)} %bitcast.13, bf16[384,2048]{1,0:T(8,128)(2,1)S(1)} %copy-done.1, bf16[384,2048]{1,0:T(8,128)(2,1)S(1)} %collective-permute-done.2.refs_2_, s32[384,1]{1,0:T(8,128)S(1)} %copy.18.refs_3_.owner_ref, ...), custom_call_target="tpu_custom_call" | custom-call | flops 322122560 | bytes 1048576 | tf_op jit(solution)/shard_map/pallas_call | solution.py:213
  23.7 10.7 %collective-permute-done.1.refs_0_ = bf16[256,2048]{1,0:T(8,128)(2,1)} collective-permute-done((bf16[256,2048]{1,0:T(8,128)(2,1)}, bf16[256,2048]{1,0:T(8,128)(2,1)}, u32[]{:S(2)}, u32[]{:S(2)}) %collective-permute-start.1) | collective-permute-done | bytes 1048608 | tf_op jit(solution)/shard_map/ppermute | solution.py:245
  34.4 1.5 %collective-permute-start.11 = (bf16[256,2048]{1,0:T(8,128)(2,1)}, bf16[256,2048]{1,0:T(8,128)(2,1)}, u32[]{:S(2)}, u32[]{:S(2)}) collective-permute-start(bf16[256,2048]{1,0:T(8,128)(2,1)} %constant_dynamic-slice_fusion.1), channel_id=1, source_target_pairs={{0,2},{2,0},{1,3},{3,1},{4,6},{6,4},{5,7},{7,5},{8,10},{10,8},{9,1... | collective-permute-start | bytes 3145736 | tf_op jit(solution)/shard_map/ppermute | solution.py:251
  35.9 1.5 %collective-permute-start.8 = (bf16[256,2048]{1,0:T(8,128)(2,1)}, bf16[256,2048]{1,0:T(8,128)(2,1)}, u32[]{:S(2)}, u32[]{:S(2)}) collective-permute-start(bf16[256,2048]{1,0:T(8,128)(2,1)} %collective-permute-done.1.refs_0_), channel_id=1, source_target_pairs={{0,16},{16,0},{1,17},{17,1},{2,18},{18,2},{3,19},{19,3},{4,20},{20... | collective-permute-start | bytes 3145736 | tf_op jit(solution)/shard_map/ppermute | solution.py:252
  37.4 1.0 collective-permute-done.refs_0_
  38.5 1.3 collective-permute-start.7
  39.8 1.8 %collective-permute-start.5 = (bf16[384,2048]{1,0:T(8,128)(2,1)}, bf16[384,2048]{1,0:T(8,128)(2,1)}, u32[]{:S(2)}, u32[]{:S(2)}) collective-permute-start(bf16[384,2048]{1,0:T(8,128)(2,1)} %collective-permute-done.refs_0_), channel_id=1, source_target_pairs={{4,8},{8,4},{5,9},{9,5},{6,10},{10,6},{7,11},{11,7},{20,24},{24,20... | collective-permute-start | bytes 4718600 | tf_op jit(solution)/shard_map/ppermute | solution.py:255
  41.6 0.9 copy-done.10
  42.5 0.9 copy-done.12
  43.4 3.4 %shard_map.57 = (f32[384,64]{1,0:T(8,128)S(1)}, f32[384,64]{1,0:T(8,128)S(1)}) custom-call(s32[1]{0:T(128)} %bitcast.6.first, bf16[256,2048]{1,0:T(8,128)(2,1)} %collective-permute-done.1.refs_0_, bf16[384,2048]{1,0:T(8,128)(2,1)S(1)} %copy-done.1, bf16[384,2048]{1,0:T(8,128)(2,1)S(1)} %collective-permute-done.2.refs_2_, ...), custom_call_target="tpu_custom_call" | custom-call | flops 161061280 | bytes 524288 | tf_op jit(solution)/shard_map/pallas_call | solution.py:213
  46.9 7.0 %shard_map.58.refs_3_ = f32[384,2048]{1,0:T(8,128)S(1)} custom-call(s32[1]{0:T(128)} %bitcast.7.row_block, bf16[384,2048]{1,0:T(8,128)(2,1)} %collective-permute-done.refs_0_, bf16[8192,2048]{1,0:T(8,128)(2,1)} %refs_2_.1, f32[384,2048]{1,0:T(8,128)S(1)} %copy-done.5), custom_call_target="tpu_custom_call" | custom-call | flops 644245120 | bytes 2936012 | tf_op jit(solution)/shard_map/pallas_call | solution.py:67
  53.9 1.7 %copy-done.2 = f32[384,2048]{1,0:T(8,128)} copy-done((f32[384,2048]{1,0:T(8,128)}, f32[384,2048]{1,0:T(8,128)S(1)}, u32[]{:S(2)}) %copy-start.2) | copy-done | bytes 3145752
  55.5 4.0 %collective-permute-done.11.rest_1_ = bf16[256,2048]{1,0:T(8,128)(2,1)} collective-permute-done((bf16[256,2048]{1,0:T(8,128)(2,1)}, bf16[256,2048]{1,0:T(8,128)(2,1)}, u32[]{:S(2)}, u32[]{:S(2)}) %collective-permute-start.11) | collective-permute-done | bytes 1048608 | tf_op jit(solution)/shard_map/ppermute | solution.py:251
  59.5 1.5 %collective-permute-start.12 = (bf16[256,2048]{1,0:T(8,128)(2,1)}, bf16[256,2048]{1,0:T(8,128)(2,1)}, u32[]{:S(2)}, u32[]{:S(2)}) collective-permute-start(bf16[256,2048]{1,0:T(8,128)(2,1)} %collective-permute-done.11.rest_1_), channel_id=1, source_target_pairs={{0,16},{16,0},{1,17},{17,1},{2,18},{18,2},{3,19},{19,3},{4,20},{20... | collective-permute-start | bytes 3145736 | tf_op jit(solution)/shard_map/ppermute | solution.py:268
  61.0 3.3 %shard_map.59 = (f32[384,64]{1,0:T(8,128)S(1)}, f32[384,64]{1,0:T(8,128)S(1)}) custom-call(s32[1]{0:T(128)} %bitcast.5.first, bf16[256,2048]{1,0:T(8,128)(2,1)} %collective-permute-done.8.refs_0_, bf16[384,2048]{1,0:T(8,128)(2,1)S(1)} %copy-done.1, bf16[384,2048]{1,0:T(8,128)(2,1)S(1)} %collective-permute-done.2.refs_2_, ...), custom_call_target="tpu_custom_call" | custom-call | flops 161061280 | bytes 524288 | tf_op jit(solution)/shard_map/pallas_call | solution.py:213
  64.4 1.3 collective-permute-done.9
  65.8 21.1 %all_to_all.5 = bf16[4,384,64]{1,2,0:T(8,128)(2,1)S(1)} all-to-all(bf16[4,384,64]{1,2,0:T(8,128)(2,1)S(1)} %broadcast_in_dim.2), channel_id=1, replica_groups=mesh['replica'=2,'tensor'=4,'adapter'=4] {'tensor'}, dimensions={0} | all-to-all | bytes 393216 | tf_op jit(solution)/shard_map/all_to_all | solution.py:263
  87.0 1.5 %collective-permute-start.10 = (bf16[384,2048]{1,0:T(8,128)(2,1)}, bf16[384,2048]{1,0:T(8,128)(2,1)}, u32[]{:S(2)}, u32[]{:S(2)}) collective-permute-start(bf16[384,2048]{1,0:T(8,128)(2,1)} %collective-permute-done.5.here), channel_id=1, source_target_pairs={{4,0},{8,12},{5,1},{9,13},{6,2},{10,14},{7,3},{11,15},{20,16},{24,... | collective-permute-start | bytes 4718600 | tf_op jit(solution)/shard_map/ppermute | solution.py:266
  89.2 8.5 %constant_dynamic-slice_fusion.weight_ref = bf16[2048,2048]{1,0:T(8,128)(2,1)} fusion(bf16[8192,2048]{1,0:T(8,128)(2,1)} %refs_2_.1, s32[]{:T(128)S(6)} %select_n.23), kind=kLoop, calls=%fused_computation.1 | loop fusion | bytes 16777220 | tf_op jit(solution)/shard_map/dynamic_slice | solution.py:275
  97.6 7.5 %shard_map.60.acc_ref = f32[384,2048]{1,0:T(8,128)S(1)} custom-call(s32[1]{0:T(128)} %bitcast.8.row_block, bf16[384,2048]{1,0:T(8,128)(2,1)} %collective-permute-done.6.refs_0_, bf16[384,2048]{1,0:T(8,128)(2,1)} %collective-permute-done.7.refs_1_, bf16[8192,2048]{1,0:T(8,128)(2,1)} %refs_2_.1, f32[384,2048]{1,0:T(8,128)S(1)} %copy-done.3), custom_call_target="tpu_custom_call" | custom-call | flops 644245120 | bytes 2936012 | tf_op jit(solution)/shard_map/pallas_call | solution.py:67
  105.3 1.6 %copy-done.8 = bf16[8,64,2048]{2,1,0:T(8,128)(2,1)S(1)} copy-done((bf16[8,64,2048]{2,1,0:T(8,128)(2,1)S(1)}, bf16[8,64,2048]{2,1,0:T(8,128)(2,1)}, u32[]{:S(2)}) %copy-start.8) | copy-done | bytes 2097176
  106.9 7.6 %shard_map.61.acc_ref = f32[384,2048]{1,0:T(8,128)S(1)} custom-call(s32[6]{0:T(128)S(1)} %stack.18.firsts, bf16[384,64]{1,0:T(8,128)(2,1)S(1)} %copy.22.low_ref, s32[384,1]{1,0:T(8,128)S(1)} %copy.18.refs_3_.owner_ref, f32[384,2048]{1,0:T(8,128)S(1)} %shard_map.60.acc_ref, bf16[512,2048]{1,0:T(8,128)(2,1)S(1)} %bitcast.16, ...), custom_call_target="tpu_custom_call" | custom-call | flops 644245120 | bytes 2936012 | tf_op jit(solution)/shard_map/pallas_call | solution.py:165
  114.5 9.1 %collective-permute-done.10.there = bf16[384,2048]{1,0:T(8,128)(2,1)} collective-permute-done((bf16[384,2048]{1,0:T(8,128)(2,1)}, bf16[384,2048]{1,0:T(8,128)(2,1)}, u32[]{:S(2)}, u32[]{:S(2)}) %collective-permute-start.10) | collective-permute-done | bytes 1572896 | tf_op jit(solution)/shard_map/ppermute | solution.py:266
  123.5 5.4 %shard_map.62 = bf16[384,2048]{1,0:T(8,128)(2,1)} custom-call(s32[1]{0:T(128)} %bitcast.inner, bf16[384,2048]{1,0:T(8,128)(2,1)} %collective-permute-done.5.here, bf16[384,2048]{1,0:T(8,128)(2,1)} %collective-permute-done.10.there, bf16[2048,2048]{1,0:T(8,128)(2,1)S(1)} %copy-done, f32[384,2048]{1,0:T(8,128)S(1)} %shard_map.61.acc_ref), custom_call_target="tpu_custom_call" | custom-call | flops 644245120 | bytes 2936012 | tf_op jit(solution)/shard_map/pallas_call | solution.py:115
  (44 shorter events, 3.8 us)
Async XLA Ops:
  0.0 10.0 %copy-start.1 = (bf16[384,2048]{1,0:T(8,128)(2,1)S(1)}, bf16[384,2048]{1,0:T(8,128)(2,1)}, u32[]{:S(2)}) copy-start(bf16[384,2048]{1,0:T(8,128)(2,1)} %refs_1_.9) | copy-start | bytes 4718596
  0.0 34.4 %collective-permute-start.4 = (bf16[512,2048]{1,0:T(8,128)(2,1)}, bf16[512,2048]{1,0:T(8,128)(2,1)}, u32[]{:S(2)}, u32[]{:S(2)}) collective-permute-start(bf16[512,2048]{1,0:T(8,128)(2,1)} %bitcast.14), channel_id=1, source_target_pairs={{0,1},{1,0},{2,3},{3,2},{4,5},{5,4},{6,7},{7,6},{8,9},{9,8},{10,11... | collective-permute-start | bytes 6291464 | tf_op jit(solution)/shard_map/ppermute | solution.py:246
  0.5 18.9 %collective-permute-start.2 = (bf16[384,2048]{1,0:T(8,128)(2,1)}, bf16[384,2048]{1,0:T(8,128)(2,1)S(1)}, u32[]{:S(2)}, u32[]{:S(2)}) collective-permute-start(bf16[384,2048]{1,0:T(8,128)(2,1)} %refs_1_.9), channel_id=1, source_target_pairs={{0,1},{1,0},{2,3},{3,2},{4,5},{5,4},{6,7},{7,6},{8,9},{9,8},{10,11... | collective-permute-start | bytes 4718600 | tf_op jit(solution)/shard_map/ppermute | solution.py:243
  0.5 38.0 %collective-permute-start = (bf16[384,2048]{1,0:T(8,128)(2,1)}, bf16[384,2048]{1,0:T(8,128)(2,1)}, u32[]{:S(2)}, u32[]{:S(2)}) collective-permute-start(bf16[384,2048]{1,0:T(8,128)(2,1)} %refs_1_.9), channel_id=1, source_target_pairs={{0,4},{4,0},{8,12},{12,8},{1,5},{5,1},{9,13},{13,9},{2,6},{6,2},{1... | collective-permute-start | bytes 4718600 | tf_op jit(solution)/shard_map/ppermute | solution.py:240
  3.5 34.9 %collective-permute-start.6 = (bf16[384,2048]{1,0:T(8,128)(2,1)}, bf16[384,2048]{1,0:T(8,128)(2,1)}, u32[]{:S(2)}, u32[]{:S(2)}) collective-permute-start(bf16[384,2048]{1,0:T(8,128)(2,1)} %refs_1_.9), channel_id=1, source_target_pairs={{4,8},{8,4},{5,9},{9,5},{6,10},{10,6},{7,11},{11,7},{20,24},{24,20... | collective-permute-start | bytes 4718600 | tf_op jit(solution)/shard_map/ppermute | solution.py:241
  6.1 2.4 %collective-permute-start.3 = (s32[384,1]{1,0:T(8,128)S(1)}, s32[384,1]{1,0:T(8,128)S(1)}, u32[]{:S(2)}, u32[]{:S(2)}) collective-permute-start(s32[384,1]{1,0:T(8,128)S(1)} %copy.18.refs_3_.owner_ref), channel_id=1, source_target_pairs={{0,1},{1,0},{2,3},{3,2},{4,5},{5,4},{6,7},{7,6},{8,9},{9,8},{10,11... | collective-permute-start | bytes 4616 | tf_op jit(solution)/shard_map/ppermute | solution.py:244
  8.5 25.9 %collective-permute-start.1 = (bf16[256,2048]{1,0:T(8,128)(2,1)}, bf16[256,2048]{1,0:T(8,128)(2,1)}, u32[]{:S(2)}, u32[]{:S(2)}) collective-permute-start(bf16[256,2048]{1,0:T(8,128)(2,1)} %constant_dynamic-slice_fusion.2), channel_id=1, source_target_pairs={{0,2},{2,0},{1,3},{3,1},{4,6},{6,4},{5,7},{7,5},{8,10},{10,8},{9,1... | collective-permute-start | bytes 3145736 | tf_op jit(solution)/shard_map/ppermute | solution.py:245
  10.0 8.2 %copy-start.7 = (bf16[8,64,2048]{2,1,0:T(8,128)(2,1)S(1)}, bf16[8,64,2048]{2,1,0:T(8,128)(2,1)}, u32[]{:S(2)}) copy-start(bf16[8,64,2048]{2,1,0:T(8,128)(2,1)} %param.8) | copy-start | bytes 6291460
  16.6 1.6 %copy-start.4 = (f32[384,2048]{1,0:T(8,128)}, f32[384,2048]{1,0:T(8,128)S(1)}, u32[]{:S(2)}) copy-start(f32[384,2048]{1,0:T(8,128)S(1)} %shard_map.55.refs_2_) | copy-start | bytes 9437188
  18.2 2.0 %copy-start.6 = (bf16[8,64,2048]{2,1,0:T(8,128)(2,1)S(1)}, bf16[8,64,2048]{2,1,0:T(8,128)(2,1)}, u32[]{:S(2)}) copy-start(bf16[8,64,2048]{2,1,0:T(8,128)(2,1)} %param.7) | copy-start | bytes 6291460
  22.4 0.7 copy-start.9
  23.1 0.7 copy-start.11
  34.4 25.1 %collective-permute-start.11 = (bf16[256,2048]{1,0:T(8,128)(2,1)}, bf16[256,2048]{1,0:T(8,128)(2,1)}, u32[]{:S(2)}, u32[]{:S(2)}) collective-permute-start(bf16[256,2048]{1,0:T(8,128)(2,1)} %constant_dynamic-slice_fusion.1), channel_id=1, source_target_pairs={{0,2},{2,0},{1,3},{3,1},{4,6},{6,4},{5,7},{7,5},{8,10},{10,8},{9,1... | collective-permute-start | bytes 3145736 | tf_op jit(solution)/shard_map/ppermute | solution.py:251
  35.9 25.1 %collective-permute-start.8 = (bf16[256,2048]{1,0:T(8,128)(2,1)}, bf16[256,2048]{1,0:T(8,128)(2,1)}, u32[]{:S(2)}, u32[]{:S(2)}) collective-permute-start(bf16[256,2048]{1,0:T(8,128)(2,1)} %collective-permute-done.1.refs_0_), channel_id=1, source_target_pairs={{0,16},{16,0},{1,17},{17,1},{2,18},{18,2},{3,19},{19,3},{4,20},{20... | collective-permute-start | bytes 3145736 | tf_op jit(solution)/shard_map/ppermute | solution.py:252
  38.5 48.5 %collective-permute-start.7 = (bf16[384,2048]{1,0:T(8,128)(2,1)}, bf16[384,2048]{1,0:T(8,128)(2,1)}, u32[]{:S(2)}, u32[]{:S(2)}) collective-permute-start(bf16[384,2048]{1,0:T(8,128)(2,1)} %collective-permute-done.6.refs_0_), channel_id=1, source_target_pairs={{4,0},{8,12},{5,1},{9,13},{6,2},{10,14},{7,3},{11,15},{20,16},{24,... | collective-permute-start | bytes 4718600 | tf_op jit(solution)/shard_map/ppermute | solution.py:257
  39.8 47.2 %collective-permute-start.5 = (bf16[384,2048]{1,0:T(8,128)(2,1)}, bf16[384,2048]{1,0:T(8,128)(2,1)}, u32[]{:S(2)}, u32[]{:S(2)}) collective-permute-start(bf16[384,2048]{1,0:T(8,128)(2,1)} %collective-permute-done.refs_0_), channel_id=1, source_target_pairs={{4,8},{8,4},{5,9},{9,5},{6,10},{10,6},{7,11},{11,7},{20,24},{24,20... | collective-permute-start | bytes 4718600 | tf_op jit(solution)/shard_map/ppermute | solution.py:255
  41.6 0.9 copy-start.10
  42.5 0.9 copy-start.12
  43.4 3.4 %copy-start.5 = (f32[384,2048]{1,0:T(8,128)S(1)}, f32[384,2048]{1,0:T(8,128)}, u32[]{:S(2)}) copy-start(f32[384,2048]{1,0:T(8,128)} %copy-done.4) | copy-start | bytes 9437188
  53.9 1.7 %copy-start.2 = (f32[384,2048]{1,0:T(8,128)}, f32[384,2048]{1,0:T(8,128)S(1)}, u32[]{:S(2)}) copy-start(f32[384,2048]{1,0:T(8,128)S(1)} %shard_map.58.refs_3_) | copy-start | bytes 9437188
  59.5 29.1 %collective-permute-start.12 = (bf16[256,2048]{1,0:T(8,128)(2,1)}, bf16[256,2048]{1,0:T(8,128)(2,1)}, u32[]{:S(2)}, u32[]{:S(2)}) collective-permute-start(bf16[256,2048]{1,0:T(8,128)(2,1)} %collective-permute-done.11.rest_1_), channel_id=1, source_target_pairs={{0,16},{16,0},{1,17},{17,1},{2,18},{18,2},{3,19},{19,3},{4,20},{20... | collective-permute-start | bytes 3145736 | tf_op jit(solution)/shard_map/ppermute | solution.py:268
  64.3 1.4 %collective-permute-start.9 = (bf16[384,64]{1,0:T(8,128)(2,1)S(1)}, bf16[384,64]{1,0:T(8,128)(2,1)S(1)}, u32[]{:S(2)}, u32[]{:S(2)}) collective-permute-start(bf16[384,64]{1,0:T(8,128)(2,1)S(1)} %convert_element_type.12), channel_id=1, source_target_pairs={{0,1},{1,0},{2,3},{3,2},{4,5},{5,4},{6,7},{7,6},{8,9},{9,8},{10,11... | collective-permute-start | bytes 147464 | tf_op jit(solution)/shard_map/ppermute | solution.py:261
  87.0 36.5 %collective-permute-start.10 = (bf16[384,2048]{1,0:T(8,128)(2,1)}, bf16[384,2048]{1,0:T(8,128)(2,1)}, u32[]{:S(2)}, u32[]{:S(2)}) collective-permute-start(bf16[384,2048]{1,0:T(8,128)(2,1)} %collective-permute-done.5.here), channel_id=1, source_target_pairs={{4,0},{8,12},{5,1},{9,13},{6,2},{10,14},{7,3},{11,15},{20,16},{24,... | collective-permute-start | bytes 4718600 | tf_op jit(solution)/shard_map/ppermute | solution.py:266
  88.5 16.7 %collective-permute-start.13 = (bf16[256,2048]{1,0:T(8,128)(2,1)}, bf16[256,2048]{1,0:T(8,128)(2,1)}, u32[]{:S(2)}, u32[]{:S(2)}) collective-permute-start(bf16[256,2048]{1,0:T(8,128)(2,1)} %collective-permute-done.11.rest_1_), channel_id=1, source_target_pairs={{0,1},{1,0},{2,3},{3,2},{4,5},{5,4},{6,7},{7,6},{8,9},{9,8},{10,11... | collective-permute-start | bytes 3145736 | tf_op jit(solution)/shard_map/ppermute | solution.py:270
  88.6 16.7 %collective-permute-start.14 = (bf16[256,2048]{1,0:T(8,128)(2,1)}, bf16[256,2048]{1,0:T(8,128)(2,1)}, u32[]{:S(2)}, u32[]{:S(2)}) collective-permute-start(bf16[256,2048]{1,0:T(8,128)(2,1)} %collective-permute-done.12.rest_2_), channel_id=1, source_target_pairs={{0,1},{1,0},{2,3},{3,2},{4,5},{5,4},{6,7},{7,6},{8,9},{9,8},{10,11... | collective-permute-start | bytes 3145736 | tf_op jit(solution)/shard_map/ppermute | solution.py:270
  89.2 8.5 %copy-start.3 = (f32[384,2048]{1,0:T(8,128)S(1)}, f32[384,2048]{1,0:T(8,128)}, u32[]{:S(2)}) copy-start(f32[384,2048]{1,0:T(8,128)} %copy-done.2) | copy-start | bytes 9437188
  105.3 1.6 %copy-start.8 = (bf16[8,64,2048]{2,1,0:T(8,128)(2,1)S(1)}, bf16[8,64,2048]{2,1,0:T(8,128)(2,1)}, u32[]{:S(2)}) copy-start(bf16[8,64,2048]{2,1,0:T(8,128)(2,1)} %param.8) | copy-start | bytes 6291460
  106.9 16.7 %copy-start = (bf16[2048,2048]{1,0:T(8,128)(2,1)S(1)}, bf16[2048,2048]{1,0:T(8,128)(2,1)}, u32[]{:S(2)}) copy-start(bf16[2048,2048]{1,0:T(8,128)(2,1)} %constant_dynamic-slice_fusion.weight_ref) | copy-start | bytes 25165828

commit v4 on v3

--- a/solution.py
+++ b/solution.py
@@ -35,15 +35,15 @@
     return adapter_of == cols
 
 
-def block_kernel(sizes, row_block, *refs):
+def block_kernel(sizes, flags, *refs):
     count = sum(sizes)
     xs, weight_ref, out_ref = refs[:count], refs[count], refs[-1]
     value = refs[count + 1][...] if len(refs) > count + 2 else 0.0
     at = i = 0
     for size in sizes:
         x = xs[i][...]
-        for other in xs[i + 1 : i + size]:
-            x += other[...]
+        if size == 2:
+            x = jnp.where(flags[1] == 1, x, xs[i + 1][...])
         value += jnp.dot(
             x, weight_ref[at : at + x.shape[1], :], preferred_element_type=jnp.float32
         )
@@ -52,7 +52,7 @@
     out_ref[...] = value.astype(out_ref.dtype)
 
 
-def add_block(acc, groups, weight, row_block, dtype=jnp.float32, share=TINY):
+def add_block(acc, groups, weight, row_block, first=0, dtype=jnp.float32, share=TINY):
     rows = groups[0][0].shape[0]
     xs = [x for group in groups for x in group]
     depth = sum(group[0].shape[1] for group in groups)
@@ -60,7 +60,7 @@
     specs = [pl.BlockSpec(x.shape, lambda n, b: (0, 0)) for x in xs]
     specs.append(pl.BlockSpec((depth, TILE), lambda n, b: (b[0], n)))
     tiles = pl.BlockSpec((rows, TILE), lambda n, b: (0, n))
-    args = [row_block.astype(jnp.int32).reshape(1), *xs, weight]
+    args = [jnp.stack([row_block, first]).astype(jnp.int32), *xs, weight]
     if acc is not None:
         specs.append(tiles)
         args.append(acc)
@@ -232,7 +232,7 @@
     down = adapter_down_factor.reshape(resident * rank, features)
     up = adapter_up_factor.reshape(resident * rank, -1)
 
-    pair, middle, outward = [(0, 1), (1, 0), (2, 3), (3, 2)], [(1, 2), (2, 1)], [(1, 0), (2, 3)]
+    pair, middle = [(0, 1), (1, 0), (2, 3), (3, 2)], [(1, 2), (2, 1)]
     second, third = jnp.where(inner, z ^ 3, z ^ 2), jnp.where(inner, z ^ 2, z ^ 3)
     halves = [me * resident, (me ^ 2) * resident + replica * (resident // 2)]
     halves.append((me ^ 2) * resident + (1 - replica) * (resident // 2))
@@ -253,8 +253,7 @@
     a1, down_mine = lax.optimization_barrier((a1, down_mine))
     lows = add_shrunk(lows, down_mine, halves[1], xs, both, rank)
     m2 = lax.ppermute(a1, "tensor", middle)
-    m1, a1 = lax.optimization_barrier((m1, a1))
-    e2 = lax.ppermute(m1, "tensor", outward)
+    e2 = lax.ppermute(m1, "tensor", pair)
     acc = add_block(acc, [[a1]], query_weight, z ^ 1)
     lows, acc = lax.optimization_barrier((lows, acc))
     lows = add_shrunk(lows, down_other, halves[2], xs, both, rank)
@@ -263,7 +262,7 @@
     shares = lax.all_to_all(shares, "tensor", 0, 0)
     low = jnp.sum(shares.astype(jnp.float32), axis=0).astype(jnp.bfloat16)
     m2, e2, low = lax.optimization_barrier((m2, e2, low))
-    e3 = lax.ppermute(m2, "tensor", outward)
+    e3 = lax.ppermute(m2, "tensor", pair)
 
     up_other = lax.ppermute(up_mine, "replica", SWAP)
     up_other, _ = lax.optimization_barrier((up_other, m2))
@@ -271,7 +270,7 @@
     across = resident - 2 * (me % 2) * resident
     ups = list(zip((up, up_mine, up_other), halves)) + list(zip(near, [h + across for h in halves]))
 
-    acc = add_block(acc, [[m1, e2]], query_weight, second)
+    acc = add_block(acc, [[m1, e2]], query_weight, second, inner.astype(jnp.int32))
     weight = lax.dynamic_slice_in_dim(query_weight, third * features, features, 0)
     acc, weight = lax.optimization_barrier((acc, weight))
     acc = add_expanded(acc, low, owners, ups)

time: 130 us -> 125 us (0.962)
  blocking collectives: 21.1 us -> 16.8 us
  waiting for transfers between devices: 26 us -> 22.1 us
  starting transfers between devices: 16.6 us -> 18.4 us
  Pallas kernels: 42.8 us -> 44.4 us
    all_to_all x1, blocking collectives: 21.1 us -> 16.8 us  [local_line(): shares = lax.all_to_all(shares, 'tensor', 0, 0)]
    ppermute x1, starting transfers between devices: 3.02 us -> 4.77 us  [local_line(): a1 = lax.ppermute(requests, 'tensor', pair)]
    ppermute x2, waiting for transfers between devices: 9.06 us -> 7.37 us  [the longest x1 7.37 us: local_line(): e3 = lax.ppermute(m2, 'tensor', pair)]
    pallas_call x3, Pallas kernels: 21 us -> 22.6 us  [add_block(): pl.pallas_call(functools.partial(block_kernel, tuple((len(group) for grou...]
  transfers between devices with their start and end apart: 15 -> 15, of which waited for: 5 -> 5; matrix products, arithmetic and copies ran while one was open for 10% -> 11% of each run, Pallas kernels for 29% -> 31%
where the time goes in v4:
time: 125 us; the launch traced here: 124 us
  Pallas kernels  44.4 us (36%)
  waiting for transfers between devices  22.1 us (18%)
  local copies, waits for them, and re-layouts  22 us (18%)
  starting transfers between devices  18.4 us (15%)
  blocking collectives  16.8 us (13%)
    pallas_call x3, Pallas kernels, add_block(): pl.pallas_call(functools.partial(block_kernel, tuple((len(group) for grou...  22.6 us
    all_to_all x1, blocking collectives, local_line(): shares = lax.all_to_all(shares, 'tensor', 0, 0)  16.8 us
    ppermute x1, waiting for transfers between devices, local_line(): down_mine = lax.ppermute(half_of(down, replica), 'adapter', ACROSS)  10.1 us
    unnamed x27, local copies, waits for them, and re-layouts  9.77 us
    pallas_call x3, Pallas kernels, add_shrunk(): pl.pallas_call(functools.partial(shrink_kernel, piece.shape[0] // rank, r...  8.81 us
    dynamic_slice x1, local copies, waits for them, and re-layouts, local_line(): lax.dynamic_slice_in_dim(query_weight, third * features, features, 0)  8.48 us
    pallas_call x1, Pallas kernels, add_expanded(): pl.pallas_call(functools.partial(expand_kernel, counts, rank), grid_spec=...  7.61 us
    ppermute x1, waiting for transfers between devices, local_line(): e3 = lax.ppermute(m2, 'tensor', pair)  7.37 us
  transfers between devices with their start and end apart: 15, of which 5 were waited for; matrix products, arithmetic and copies ran while one was open for 11% of the time, Pallas kernels for 31%

profile of v4, /device:TPU:0, one launch (start us, length us, event | category | flops | bytes accessed | tf_op | source)
XLA Modules:
  0.0 124.4 jit_solution(8846288000854593391)
XLA Ops:
  0.5 1.8 %collective-permute-start.6 = (bf16[384,2048]{1,0:T(8,128)(2,1)}, bf16[384,2048]{1,0:T(8,128)(2,1)}, u32[]{:S(2)}, u32[]{:S(2)}) collective-permute-start(bf16[384,2048]{1,0:T(8,128)(2,1)} %refs_1_.9), channel_id=1, source_target_pairs={{4,8},{8,4},{5,9},{9,5},{6,10},{10,6},{7,11},{11,7},{20,24},{24,20... | collective-permute-start | bytes 4718600 | tf_op jit(solution)/shard_map/ppermute | solution.py:241
  2.3 4.8 %collective-permute-start = (bf16[384,2048]{1,0:T(8,128)(2,1)}, bf16[384,2048]{1,0:T(8,128)(2,1)}, u32[]{:S(2)}, u32[]{:S(2)}) collective-permute-start(bf16[384,2048]{1,0:T(8,128)(2,1)} %refs_1_.9), channel_id=1, source_target_pairs={{0,4},{4,0},{8,12},{12,8},{1,5},{5,1},{9,13},{13,9},{2,6},{6,2},{1... | collective-permute-start | bytes 4718600 | tf_op jit(solution)/shard_map/ppermute | solution.py:240
  7.1 0.8 copy.18.refs_3_.owner_ref
  8.0 2.3 %constant_dynamic-slice_fusion.2 = bf16[256,2048]{1,0:T(8,128)(2,1)} fusion(bf16[512,2048]{1,0:T(8,128)(2,1)} %bitcast.12, s32[]{:T(128)S(6)} %select_n.20), kind=kLoop, calls=%fused_computation.3 | loop fusion | bytes 2097156 | tf_op jit(solution)/shard_map/dynamic_slice | solution.py:192
  10.3 1.5 %collective-permute-start.1 = (bf16[256,2048]{1,0:T(8,128)(2,1)}, bf16[256,2048]{1,0:T(8,128)(2,1)}, u32[]{:S(2)}, u32[]{:S(2)}) collective-permute-start(bf16[256,2048]{1,0:T(8,128)(2,1)} %constant_dynamic-slice_fusion.2), channel_id=1, source_target_pairs={{0,2},{2,0},{1,3},{3,1},{4,6},{6,4},{5,7},{7,5},{8,10},{10,8},{9,1... | collective-permute-start | bytes 3145736 | tf_op jit(solution)/shard_map/ppermute | solution.py:245
  11.9 7.0 %shard_map.55.refs_2_ = f32[384,2048]{1,0:T(8,128)S(1)} custom-call(s32[2]{0:T(128)S(1)} %pad_add_fusion.1.flags, bf16[384,2048]{1,0:T(8,128)(2,1)S(1)} %copy-done.1, bf16[8192,2048]{1,0:T(8,128)(2,1)} %refs_2_.1), custom_call_target="tpu_custom_call" | custom-call | flops 644245120 | bytes 2936012 | tf_op jit(solution)/shard_map/pallas_call | solution.py:67
  18.9 1.6 %copy-done.4 = f32[384,2048]{1,0:T(8,128)} copy-done((f32[384,2048]{1,0:T(8,128)}, f32[384,2048]{1,0:T(8,128)S(1)}, u32[]{:S(2)}) %copy-start.4) | copy-done | bytes 3145752
  20.6 1.1 constant_dynamic-slice_fusion.1
  21.7 0.8 copy-done.6
  22.5 2.2 %shard_map.56 = (f32[384,64]{1,0:T(8,128)S(1)}, f32[384,64]{1,0:T(8,128)S(1)}) custom-call(s32[1]{0:T(128)} %bitcast.3.first, bf16[512,2048]{1,0:T(8,128)(2,1)S(1)} %bitcast.13, bf16[384,2048]{1,0:T(8,128)(2,1)S(1)} %copy-done.1, bf16[384,2048]{1,0:T(8,128)(2,1)S(1)} %collective-permute-done.2.refs_2_, s32[384,1]{1,0:T(8,128)S(1)} %copy.18.refs_3_.owner_ref, ...), custom_call_target="tpu_custom_call" | custom-call | flops 322122560 | bytes 1048576 | tf_op jit(solution)/shard_map/pallas_call | solution.py:213
  24.7 0.7 copy-done.9
  26.1 10.1 %collective-permute-done.1.refs_0_ = bf16[256,2048]{1,0:T(8,128)(2,1)} collective-permute-done((bf16[256,2048]{1,0:T(8,128)(2,1)}, bf16[256,2048]{1,0:T(8,128)(2,1)}, u32[]{:S(2)}, u32[]{:S(2)}) %collective-permute-start.1) | collective-permute-done | bytes 1048608 | tf_op jit(solution)/shard_map/ppermute | solution.py:245
  36.2 1.5 %collective-permute-start.11 = (bf16[256,2048]{1,0:T(8,128)(2,1)}, bf16[256,2048]{1,0:T(8,128)(2,1)}, u32[]{:S(2)}, u32[]{:S(2)}) collective-permute-start(bf16[256,2048]{1,0:T(8,128)(2,1)} %constant_dynamic-slice_fusion.1), channel_id=1, source_target_pairs={{0,2},{2,0},{1,3},{3,1},{4,6},{6,4},{5,7},{7,5},{8,10},{10,8},{9,1... | collective-permute-start | bytes 3145736 | tf_op jit(solution)/shard_map/ppermute | solution.py:251
  37.7 1.5 %collective-permute-start.8 = (bf16[256,2048]{1,0:T(8,128)(2,1)}, bf16[256,2048]{1,0:T(8,128)(2,1)}, u32[]{:S(2)}, u32[]{:S(2)}) collective-permute-start(bf16[256,2048]{1,0:T(8,128)(2,1)} %collective-permute-done.1.refs_0_), channel_id=1, source_target_pairs={{0,16},{16,0},{1,17},{17,1},{2,18},{18,2},{3,19},{19,3},{4,20},{20... | collective-permute-start | bytes 3145736 | tf_op jit(solution)/shard_map/ppermute | solution.py:252
  39.2 2.9 %collective-permute-start.7 = (bf16[384,2048]{1,0:T(8,128)(2,1)}, bf16[384,2048]{1,0:T(8,128)(2,1)}, u32[]{:S(2)}, u32[]{:S(2)}) collective-permute-start(bf16[384,2048]{1,0:T(8,128)(2,1)} %collective-permute-done.6.refs_0_), channel_id=1, source_target_pairs={{0,4},{4,0},{8,12},{12,8},{1,5},{5,1},{9,13},{13,9},{2,6},{6,2},{1... | collective-permute-start | bytes 4718600 | tf_op jit(solution)/shard_map/ppermute | solution.py:256
  42.1 1.8 %collective-permute-start.5 = (bf16[384,2048]{1,0:T(8,128)(2,1)}, bf16[384,2048]{1,0:T(8,128)(2,1)}, u32[]{:S(2)}, u32[]{:S(2)}) collective-permute-start(bf16[384,2048]{1,0:T(8,128)(2,1)} %collective-permute-done.refs_0_), channel_id=1, source_target_pairs={{4,8},{8,4},{5,9},{9,5},{6,10},{10,6},{7,11},{11,7},{20,24},{24,20... | collective-permute-start | bytes 4718600 | tf_op jit(solution)/shard_map/ppermute | solution.py:255
  44.0 0.9 copy-done.10
  44.9 0.9 copy-done.12
  45.8 3.4 %shard_map.57 = (f32[384,64]{1,0:T(8,128)S(1)}, f32[384,64]{1,0:T(8,128)S(1)}) custom-call(s32[1]{0:T(128)} %bitcast.6.first, bf16[256,2048]{1,0:T(8,128)(2,1)} %collective-permute-done.1.refs_0_, bf16[384,2048]{1,0:T(8,128)(2,1)S(1)} %copy-done.1, bf16[384,2048]{1,0:T(8,128)(2,1)S(1)} %collective-permute-done.2.refs_2_, ...), custom_call_target="tpu_custom_call" | custom-call | flops 161061280 | bytes 524288 | tf_op jit(solution)/shard_map/pallas_call | solution.py:213
  49.3 7.5 %shard_map.58.refs_3_ = f32[384,2048]{1,0:T(8,128)S(1)} custom-call(s32[2]{0:T(128)S(1)} %pad_add_fusion.flags, bf16[384,2048]{1,0:T(8,128)(2,1)} %collective-permute-done.refs_0_, bf16[8192,2048]{1,0:T(8,128)(2,1)} %refs_2_.1, f32[384,2048]{1,0:T(8,128)S(1)} %copy-done.5), custom_call_target="tpu_custom_call" | custom-call | flops 644245120 | bytes 2936012 | tf_op jit(solution)/shard_map/pallas_call | solution.py:67
  56.8 1.7 %copy-done.2 = f32[384,2048]{1,0:T(8,128)} copy-done((f32[384,2048]{1,0:T(8,128)}, f32[384,2048]{1,0:T(8,128)S(1)}, u32[]{:S(2)}) %copy-start.2) | copy-done | bytes 3145752
  58.5 2.8 %collective-permute-done.11.rest_1_ = bf16[256,2048]{1,0:T(8,128)(2,1)} collective-permute-done((bf16[256,2048]{1,0:T(8,128)(2,1)}, bf16[256,2048]{1,0:T(8,128)(2,1)}, u32[]{:S(2)}, u32[]{:S(2)}) %collective-permute-start.11) | collective-permute-done | bytes 1048608 | tf_op jit(solution)/shard_map/ppermute | solution.py:251
  61.3 1.5 %collective-permute-start.12 = (bf16[256,2048]{1,0:T(8,128)(2,1)}, bf16[256,2048]{1,0:T(8,128)(2,1)}, u32[]{:S(2)}, u32[]{:S(2)}) collective-permute-start(bf16[256,2048]{1,0:T(8,128)(2,1)} %collective-permute-done.11.rest_1_), channel_id=1, source_target_pairs={{0,16},{16,0},{1,17},{17,1},{2,18},{18,2},{3,19},{19,3},{4,20},{20... | collective-permute-start | bytes 3145736 | tf_op jit(solution)/shard_map/ppermute | solution.py:267
  62.8 3.3 %shard_map.59 = (f32[384,64]{1,0:T(8,128)S(1)}, f32[384,64]{1,0:T(8,128)S(1)}) custom-call(s32[1]{0:T(128)} %bitcast.5.first, bf16[256,2048]{1,0:T(8,128)(2,1)} %collective-permute-done.8.refs_0_, bf16[384,2048]{1,0:T(8,128)(2,1)S(1)} %copy-done.1, bf16[384,2048]{1,0:T(8,128)(2,1)S(1)} %collective-permute-done.2.refs_2_, ...), custom_call_target="tpu_custom_call" | custom-call | flops 161061280 | bytes 524288 | tf_op jit(solution)/shard_map/pallas_call | solution.py:213
  66.1 1.3 %collective-permute-done.9 = bf16[384,64]{1,0:T(8,128)(2,1)S(1)} collective-permute-done((bf16[384,64]{1,0:T(8,128)(2,1)S(1)}, bf16[384,64]{1,0:T(8,128)(2,1)S(1)}, u32[]{:S(2)}, u32[]{:S(2)}) %collective-permute-start.9) | collective-permute-done | bytes 49184 | tf_op jit(solution)/shard_map/ppermute | solution.py:260
  67.6 16.8 %all_to_all.5 = bf16[4,384,64]{1,2,0:T(8,128)(2,1)S(1)} all-to-all(bf16[4,384,64]{1,2,0:T(8,128)(2,1)S(1)} %broadcast_in_dim.2), channel_id=1, replica_groups=mesh['replica'=2,'tensor'=4,'adapter'=4] {'tensor'}, dimensions={0} | all-to-all | bytes 393216 | tf_op jit(solution)/shard_map/all_to_all | solution.py:262
  85.6 8.5 %constant_dynamic-slice_fusion.weight_ref = bf16[2048,2048]{1,0:T(8,128)(2,1)} fusion(bf16[8192,2048]{1,0:T(8,128)(2,1)} %refs_2_.1, s32[]{:T(128)S(6)} %select_n.23), kind=kLoop, calls=%fused_computation.1 | loop fusion | bytes 16777220 | tf_op jit(solution)/shard_map/dynamic_slice | solution.py:274
  94.1 8.0 %shard_map.60.acc_ref = f32[384,2048]{1,0:T(8,128)S(1)} custom-call(s32[2]{0:T(128)S(1)} %pad_add_fusion.2.flags, bf16[384,2048]{1,0:T(8,128)(2,1)} %collective-permute-done.6.refs_0_, bf16[384,2048]{1,0:T(8,128)(2,1)} %collective-permute-done.7.refs_1_, bf16[8192,2048]{1,0:T(8,128)(2,1)} %refs_2_.1, f32[384,2048]{1,0:T(8,128)S(1)} %copy-done.3), custom_call_target="tpu_custom_call" | custom-call | flops 644245120 | bytes 2936012 | tf_op jit(solution)/shard_map/pallas_call | solution.py:67
  102.3 1.6 %copy-done.8 = bf16[8,64,2048]{2,1,0:T(8,128)(2,1)S(1)} copy-done((bf16[8,64,2048]{2,1,0:T(8,128)(2,1)S(1)}, bf16[8,64,2048]{2,1,0:T(8,128)(2,1)}, u32[]{:S(2)}) %copy-start.8) | copy-done | bytes 2097176
  103.9 7.6 %shard_map.61.acc_ref = f32[384,2048]{1,0:T(8,128)S(1)} custom-call(s32[6]{0:T(128)S(1)} %stack.43.firsts, bf16[384,64]{1,0:T(8,128)(2,1)S(1)} %copy.22.low_ref, s32[384,1]{1,0:T(8,128)S(1)} %copy.18.refs_3_.owner_ref, f32[384,2048]{1,0:T(8,128)S(1)} %shard_map.60.acc_ref, bf16[512,2048]{1,0:T(8,128)(2,1)S(1)} %bitcast.16, ...), custom_call_target="tpu_custom_call" | custom-call | flops 644245120 | bytes 2936012 | tf_op jit(solution)/shard_map/pallas_call | solution.py:165
  111.5 7.4 %collective-permute-done.10.there = bf16[384,2048]{1,0:T(8,128)(2,1)} collective-permute-done((bf16[384,2048]{1,0:T(8,128)(2,1)}, bf16[384,2048]{1,0:T(8,128)(2,1)}, u32[]{:S(2)}, u32[]{:S(2)}) %collective-permute-start.10) | collective-permute-done | bytes 1572896 | tf_op jit(solution)/shard_map/ppermute | solution.py:265
  118.9 5.4 %shard_map.62 = bf16[384,2048]{1,0:T(8,128)(2,1)} custom-call(s32[1]{0:T(128)} %bitcast.inner, bf16[384,2048]{1,0:T(8,128)(2,1)} %collective-permute-done.5.here, bf16[384,2048]{1,0:T(8,128)(2,1)} %collective-permute-done.10.there, bf16[2048,2048]{1,0:T(8,128)(2,1)S(1)} %copy-done, f32[384,2048]{1,0:T(8,128)S(1)} %shard_map.61.acc_ref), custom_call_target="tpu_custom_call" | custom-call | flops 644245120 | bytes 2936012 | tf_op jit(solution)/shard_map/pallas_call | solution.py:115
  (47 shorter events, 3.0 us)
Async XLA Ops:
  0.0 11.9 %copy-start.1 = (bf16[384,2048]{1,0:T(8,128)(2,1)S(1)}, bf16[384,2048]{1,0:T(8,128)(2,1)}, u32[]{:S(2)}) copy-start(bf16[384,2048]{1,0:T(8,128)(2,1)} %refs_1_.9) | copy-start | bytes 4718596
  0.0 36.2 %collective-permute-start.4 = (bf16[512,2048]{1,0:T(8,128)(2,1)}, bf16[512,2048]{1,0:T(8,128)(2,1)}, u32[]{:S(2)}, u32[]{:S(2)}) collective-permute-start(bf16[512,2048]{1,0:T(8,128)(2,1)} %bitcast.14), channel_id=1, source_target_pairs={{0,1},{1,0},{2,3},{3,2},{4,5},{5,4},{6,7},{7,6},{8,9},{9,8},{10,11... | collective-permute-start | bytes 6291464 | tf_op jit(solution)/shard_map/ppermute | solution.py:246
  0.5 21.2 %collective-permute-start.2 = (bf16[384,2048]{1,0:T(8,128)(2,1)}, bf16[384,2048]{1,0:T(8,128)(2,1)S(1)}, u32[]{:S(2)}, u32[]{:S(2)}) collective-permute-start(bf16[384,2048]{1,0:T(8,128)(2,1)} %refs_1_.9), channel_id=1, source_target_pairs={{0,1},{1,0},{2,3},{3,2},{4,5},{5,4},{6,7},{7,6},{8,9},{9,8},{10,11... | collective-permute-start | bytes 4718600 | tf_op jit(solution)/shard_map/ppermute | solution.py:243
  0.5 38.7 %collective-permute-start.6 = (bf16[384,2048]{1,0:T(8,128)(2,1)}, bf16[384,2048]{1,0:T(8,128)(2,1)}, u32[]{:S(2)}, u32[]{:S(2)}) collective-permute-start(bf16[384,2048]{1,0:T(8,128)(2,1)} %refs_1_.9), channel_id=1, source_target_pairs={{4,8},{8,4},{5,9},{9,5},{6,10},{10,6},{7,11},{11,7},{20,24},{24,20... | collective-permute-start | bytes 4718600 | tf_op jit(solution)/shard_map/ppermute | solution.py:241
  2.3 39.8 %collective-permute-start = (bf16[384,2048]{1,0:T(8,128)(2,1)}, bf16[384,2048]{1,0:T(8,128)(2,1)}, u32[]{:S(2)}, u32[]{:S(2)}) collective-permute-start(bf16[384,2048]{1,0:T(8,128)(2,1)} %refs_1_.9), channel_id=1, source_target_pairs={{0,4},{4,0},{8,12},{12,8},{1,5},{5,1},{9,13},{13,9},{2,6},{6,2},{1... | collective-permute-start | bytes 4718600 | tf_op jit(solution)/shard_map/ppermute | solution.py:240
  7.9 2.4 %collective-permute-start.3 = (s32[384,1]{1,0:T(8,128)S(1)}, s32[384,1]{1,0:T(8,128)S(1)}, u32[]{:S(2)}, u32[]{:S(2)}) collective-permute-start(s32[384,1]{1,0:T(8,128)S(1)} %copy.18.refs_3_.owner_ref), channel_id=1, source_target_pairs={{0,1},{1,0},{2,3},{3,2},{4,5},{5,4},{6,7},{7,6},{8,9},{9,8},{10,11... | collective-permute-start | bytes 4616 | tf_op jit(solution)/shard_map/ppermute | solution.py:244
  10.3 25.9 %collective-permute-start.1 = (bf16[256,2048]{1,0:T(8,128)(2,1)}, bf16[256,2048]{1,0:T(8,128)(2,1)}, u32[]{:S(2)}, u32[]{:S(2)}) collective-permute-start(bf16[256,2048]{1,0:T(8,128)(2,1)} %constant_dynamic-slice_fusion.2), channel_id=1, source_target_pairs={{0,2},{2,0},{1,3},{3,1},{4,6},{6,4},{5,7},{7,5},{8,10},{10,8},{9,1... | collective-permute-start | bytes 3145736 | tf_op jit(solution)/shard_map/ppermute | solution.py:245
  11.9 8.7 %copy-start.7 = (bf16[8,64,2048]{2,1,0:T(8,128)(2,1)S(1)}, bf16[8,64,2048]{2,1,0:T(8,128)(2,1)}, u32[]{:S(2)}) copy-start(bf16[8,64,2048]{2,1,0:T(8,128)(2,1)} %param.8) | copy-start | bytes 6291460
  18.9 1.6 %copy-start.4 = (f32[384,2048]{1,0:T(8,128)}, f32[384,2048]{1,0:T(8,128)S(1)}, u32[]{:S(2)}) copy-start(f32[384,2048]{1,0:T(8,128)S(1)} %shard_map.55.refs_2_) | copy-start | bytes 9437188
  20.5 2.0 %copy-start.6 = (bf16[8,64,2048]{2,1,0:T(8,128)(2,1)S(1)}, bf16[8,64,2048]{2,1,0:T(8,128)(2,1)}, u32[]{:S(2)}) copy-start(bf16[8,64,2048]{2,1,0:T(8,128)(2,1)} %param.7) | copy-start | bytes 6291460
  24.7 0.7 copy-start.9
  25.4 0.7 copy-start.11
  36.2 25.1 %collective-permute-start.11 = (bf16[256,2048]{1,0:T(8,128)(2,1)}, bf16[256,2048]{1,0:T(8,128)(2,1)}, u32[]{:S(2)}, u32[]{:S(2)}) collective-permute-start(bf16[256,2048]{1,0:T(8,128)(2,1)} %constant_dynamic-slice_fusion.1), channel_id=1, source_target_pairs={{0,2},{2,0},{1,3},{3,1},{4,6},{6,4},{5,7},{7,5},{8,10},{10,8},{9,1... | collective-permute-start | bytes 3145736 | tf_op jit(solution)/shard_map/ppermute | solution.py:251
  37.7 25.1 %collective-permute-start.8 = (bf16[256,2048]{1,0:T(8,128)(2,1)}, bf16[256,2048]{1,0:T(8,128)(2,1)}, u32[]{:S(2)}, u32[]{:S(2)}) collective-permute-start(bf16[256,2048]{1,0:T(8,128)(2,1)} %collective-permute-done.1.refs_0_), channel_id=1, source_target_pairs={{0,16},{16,0},{1,17},{17,1},{2,18},{18,2},{3,19},{19,3},{4,20},{20... | collective-permute-start | bytes 3145736 | tf_op jit(solution)/shard_map/ppermute | solution.py:252
  39.2 45.3 %collective-permute-start.7 = (bf16[384,2048]{1,0:T(8,128)(2,1)}, bf16[384,2048]{1,0:T(8,128)(2,1)}, u32[]{:S(2)}, u32[]{:S(2)}) collective-permute-start(bf16[384,2048]{1,0:T(8,128)(2,1)} %collective-permute-done.6.refs_0_), channel_id=1, source_target_pairs={{0,4},{4,0},{8,12},{12,8},{1,5},{5,1},{9,13},{13,9},{2,6},{6,2},{1... | collective-permute-start | bytes 4718600 | tf_op jit(solution)/shard_map/ppermute | solution.py:256
  42.1 42.4 %collective-permute-start.5 = (bf16[384,2048]{1,0:T(8,128)(2,1)}, bf16[384,2048]{1,0:T(8,128)(2,1)}, u32[]{:S(2)}, u32[]{:S(2)}) collective-permute-start(bf16[384,2048]{1,0:T(8,128)(2,1)} %collective-permute-done.refs_0_), channel_id=1, source_target_pairs={{4,8},{8,4},{5,9},{9,5},{6,10},{10,6},{7,11},{11,7},{20,24},{24,20... | collective-permute-start | bytes 4718600 | tf_op jit(solution)/shard_map/ppermute | solution.py:255
  44.0 0.9 copy-start.10
  44.9 0.9 copy-start.12
  45.8 3.4 %copy-start.5 = (f32[384,2048]{1,0:T(8,128)S(1)}, f32[384,2048]{1,0:T(8,128)}, u32[]{:S(2)}) copy-start(f32[384,2048]{1,0:T(8,128)} %copy-done.4) | copy-start | bytes 9437188
  56.8 1.7 %copy-start.2 = (f32[384,2048]{1,0:T(8,128)}, f32[384,2048]{1,0:T(8,128)S(1)}, u32[]{:S(2)}) copy-start(f32[384,2048]{1,0:T(8,128)S(1)} %shard_map.58.refs_3_) | copy-start | bytes 9437188
  61.3 24.2 %collective-permute-start.12 = (bf16[256,2048]{1,0:T(8,128)(2,1)}, bf16[256,2048]{1,0:T(8,128)(2,1)}, u32[]{:S(2)}, u32[]{:S(2)}) collective-permute-start(bf16[256,2048]{1,0:T(8,128)(2,1)} %collective-permute-done.11.rest_1_), channel_id=1, source_target_pairs={{0,16},{16,0},{1,17},{17,1},{2,18},{18,2},{3,19},{19,3},{4,20},{20... | collective-permute-start | bytes 3145736 | tf_op jit(solution)/shard_map/ppermute | solution.py:267
  66.1 1.4 %collective-permute-start.9 = (bf16[384,64]{1,0:T(8,128)(2,1)S(1)}, bf16[384,64]{1,0:T(8,128)(2,1)S(1)}, u32[]{:S(2)}, u32[]{:S(2)}) collective-permute-start(bf16[384,64]{1,0:T(8,128)(2,1)S(1)} %convert_element_type.6), channel_id=1, source_target_pairs={{0,1},{1,0},{2,3},{3,2},{4,5},{5,4},{6,7},{7,6},{8,9},{9,8},{10,11... | collective-permute-start | bytes 147464 | tf_op jit(solution)/shard_map/ppermute | solution.py:260
  84.5 34.4 %collective-permute-start.10 = (bf16[384,2048]{1,0:T(8,128)(2,1)}, bf16[384,2048]{1,0:T(8,128)(2,1)}, u32[]{:S(2)}, u32[]{:S(2)}) collective-permute-start(bf16[384,2048]{1,0:T(8,128)(2,1)} %collective-permute-done.5.here), channel_id=1, source_target_pairs={{0,4},{4,0},{8,12},{12,8},{1,5},{5,1},{9,13},{13,9},{2,6},{6,2},{1... | collective-permute-start | bytes 4718600 | tf_op jit(solution)/shard_map/ppermute | solution.py:265
  84.9 17.3 %collective-permute-start.13 = (bf16[256,2048]{1,0:T(8,128)(2,1)}, bf16[256,2048]{1,0:T(8,128)(2,1)}, u32[]{:S(2)}, u32[]{:S(2)}) collective-permute-start(bf16[256,2048]{1,0:T(8,128)(2,1)} %collective-permute-done.11.rest_1_), channel_id=1, source_target_pairs={{0,1},{1,0},{2,3},{3,2},{4,5},{5,4},{6,7},{7,6},{8,9},{9,8},{10,11... | collective-permute-start | bytes 3145736 | tf_op jit(solution)/shard_map/ppermute | solution.py:269
  85.5 16.8 %collective-permute-start.14 = (bf16[256,2048]{1,0:T(8,128)(2,1)}, bf16[256,2048]{1,0:T(8,128)(2,1)}, u32[]{:S(2)}, u32[]{:S(2)}) collective-permute-start(bf16[256,2048]{1,0:T(8,128)(2,1)} %collective-permute-done.12.rest_2_), channel_id=1, source_target_pairs={{0,1},{1,0},{2,3},{3,2},{4,5},{5,4},{6,7},{7,6},{8,9},{9,8},{10,11... | collective-permute-start | bytes 3145736 | tf_op jit(solution)/shard_map/ppermute | solution.py:269
  85.6 8.5 %copy-start.3 = (f32[384,2048]{1,0:T(8,128)S(1)}, f32[384,2048]{1,0:T(8,128)}, u32[]{:S(2)}) copy-start(f32[384,2048]{1,0:T(8,128)} %copy-done.2) | copy-start | bytes 9437188
  102.3 1.6 %copy-start.8 = (bf16[8,64,2048]{2,1,0:T(8,128)(2,1)S(1)}, bf16[8,64,2048]{2,1,0:T(8,128)(2,1)}, u32[]{:S(2)}) copy-start(bf16[8,64,2048]{2,1,0:T(8,128)(2,1)} %param.8) | copy-start | bytes 6291460
  103.9 15.0 %copy-start = (bf16[2048,2048]{1,0:T(8,128)(2,1)S(1)}, bf16[2048,2048]{1,0:T(8,128)(2,1)}, u32[]{:S(2)}) copy-start(bf16[2048,2048]{1,0:T(8,128)(2,1)} %constant_dynamic-slice_fusion.weight_ref) | copy-start | bytes 25165828

commit v5 on v4

--- a/solution.py
+++ b/solution.py
@@ -258,9 +258,10 @@
     lows, acc = lax.optimization_barrier((lows, acc))
     lows = add_shrunk(lows, down_other, halves[2], xs, both, rank)
     low = lows[0] + lax.ppermute(lows[1].astype(jnp.bfloat16), "adapter", BESIDE).astype(jnp.float32)
-    shares = jnp.broadcast_to(low.astype(jnp.bfloat16)[None], (4, *low.shape))
+    low = low.T.astype(jnp.bfloat16)
+    shares = jnp.broadcast_to(low[None], (4, *low.shape))
     shares = lax.all_to_all(shares, "tensor", 0, 0)
-    low = jnp.sum(shares.astype(jnp.float32), axis=0).astype(jnp.bfloat16)
+    low = jnp.sum(shares.astype(jnp.float32), axis=0).astype(jnp.bfloat16).T
     m2, e2, low = lax.optimization_barrier((m2, e2, low))
     e3 = lax.ppermute(m2, "tensor", pair)
 

time: 125 us -> 124 us (level)
  local copies, waits for them, and re-layouts: 22 us -> 20.5 us
  waiting for transfers between devices: 22.1 us -> 23.6 us
    ppermute x1, waiting for transfers between devices: 7.37 us -> 9.07 us  [local_line(): e3 = lax.ppermute(m2, 'tensor', pair)]
    unnamed x27, local copies, waits for them, and re-layouts: 9.77 us -> 8.23 us
  transfers between devices with their start and end apart: 15 -> 15, of which waited for: 5 -> 5; matrix products, arithmetic and copies ran while one was open for 11% -> 11% of each run, Pallas kernels for 31% -> 32%
where the time goes in v5:
time: 124 us; the launch traced here: 123 us
  Pallas kernels  43.4 us (35%)
  waiting for transfers between devices  23.6 us (19%)
  local copies, waits for them, and re-layouts  20.5 us (17%)
  starting transfers between devices  18.5 us (15%)
  blocking collectives  16.8 us (14%)
    pallas_call x3, Pallas kernels, add_block(): pl.pallas_call(functools.partial(block_kernel, tuple((len(group) for grou...  22.6 us
    all_to_all x1, blocking collectives, local_line(): shares = lax.all_to_all(shares, 'tensor', 0, 0)  16.8 us
    ppermute x1, waiting for transfers between devices, local_line(): down_mine = lax.ppermute(half_of(down, replica), 'adapter', ACROSS)  10.1 us
    ppermute x1, waiting for transfers between devices, local_line(): e3 = lax.ppermute(m2, 'tensor', pair)  9.07 us
    pallas_call x3, Pallas kernels, add_shrunk(): pl.pallas_call(functools.partial(shrink_kernel, piece.shape[0] // rank, r...  8.81 us
    dynamic_slice x1, local copies, waits for them, and re-layouts, local_line(): lax.dynamic_slice_in_dim(query_weight, third * features, features, 0)  8.48 us
    unnamed x27, local copies, waits for them, and re-layouts  8.23 us
    pallas_call x1, Pallas kernels, add_expanded(): pl.pallas_call(functools.partial(expand_kernel, counts, rank), grid_spec=...  7.44 us
  transfers between devices with their start and end apart: 15, of which 5 were waited for; matrix products, arithmetic and copies ran while one was open for 11% of the time, Pallas kernels for 32%

profile of v5, /device:TPU:0, one launch (start us, length us, event | category | flops | bytes accessed | tf_op | source)
XLA Modules:
  0.0 123.4 jit_solution(18223646238755088152)
XLA Ops:
  0.5 1.8 %collective-permute-start.6 = (bf16[384,2048]{1,0:T(8,128)(2,1)}, bf16[384,2048]{1,0:T(8,128)(2,1)}, u32[]{:S(2)}, u32[]{:S(2)}) collective-permute-start(bf16[384,2048]{1,0:T(8,128)(2,1)} %refs_1_.9), channel_id=1, source_target_pairs={{4,8},{8,4},{5,9},{9,5},{6,10},{10,6},{7,11},{11,7},{20,24},{24,20... | collective-permute-start | bytes 4718600 | tf_op jit(solution)/shard_map/ppermute | solution.py:241
  2.3 4.8 %collective-permute-start = (bf16[384,2048]{1,0:T(8,128)(2,1)}, bf16[384,2048]{1,0:T(8,128)(2,1)}, u32[]{:S(2)}, u32[]{:S(2)}) collective-permute-start(bf16[384,2048]{1,0:T(8,128)(2,1)} %refs_1_.9), channel_id=1, source_target_pairs={{0,4},{4,0},{8,12},{12,8},{1,5},{5,1},{9,13},{13,9},{2,6},{6,2},{1... | collective-permute-start | bytes 4718600 | tf_op jit(solution)/shard_map/ppermute | solution.py:240
  7.1 0.8 copy.13.refs_3_.owner_ref
  8.0 2.3 %constant_dynamic-slice_fusion.2 = bf16[256,2048]{1,0:T(8,128)(2,1)} fusion(bf16[512,2048]{1,0:T(8,128)(2,1)} %bitcast.15, s32[]{:T(128)S(6)} %select_n.20), kind=kLoop, calls=%fused_computation.4 | loop fusion | bytes 2097156 | tf_op jit(solution)/shard_map/dynamic_slice | solution.py:192
  10.3 1.5 %collective-permute-start.1 = (bf16[256,2048]{1,0:T(8,128)(2,1)}, bf16[256,2048]{1,0:T(8,128)(2,1)}, u32[]{:S(2)}, u32[]{:S(2)}) collective-permute-start(bf16[256,2048]{1,0:T(8,128)(2,1)} %constant_dynamic-slice_fusion.2), channel_id=1, source_target_pairs={{0,2},{2,0},{1,3},{3,1},{4,6},{6,4},{5,7},{7,5},{8,10},{10,8},{9,1... | collective-permute-start | bytes 3145736 | tf_op jit(solution)/shard_map/ppermute | solution.py:245
  11.9 7.0 %shard_map.55.refs_2_ = f32[384,2048]{1,0:T(8,128)S(1)} custom-call(s32[2]{0:T(128)S(1)} %pad_add_fusion.1.flags, bf16[384,2048]{1,0:T(8,128)(2,1)S(1)} %copy-done.1, bf16[8192,2048]{1,0:T(8,128)(2,1)} %refs_2_.1), custom_call_target="tpu_custom_call" | custom-call | flops 644245120 | bytes 2936012 | tf_op jit(solution)/shard_map/pallas_call | solution.py:67
  18.9 1.6 %copy-done.4 = f32[384,2048]{1,0:T(8,128)} copy-done((f32[384,2048]{1,0:T(8,128)}, f32[384,2048]{1,0:T(8,128)S(1)}, u32[]{:S(2)}) %copy-start.4) | copy-done | bytes 3145752
  20.6 1.1 constant_dynamic-slice_fusion.1
  21.7 0.9 copy-done.6
  22.5 2.1 %shard_map.56 = (f32[384,64]{1,0:T(8,128)S(1)}, f32[384,64]{1,0:T(8,128)S(1)}) custom-call(s32[1]{0:T(128)} %bitcast.3.first, bf16[512,2048]{1,0:T(8,128)(2,1)S(1)} %bitcast.16, bf16[384,2048]{1,0:T(8,128)(2,1)S(1)} %copy-done.1, bf16[384,2048]{1,0:T(8,128)(2,1)S(1)} %collective-permute-done.2.refs_2_, s32[384,1]{1,0:T(8,128)S(1)} %copy.13.refs_3_.owner_ref, ...), custom_call_target="tpu_custom_call" | custom-call | flops 322122560 | bytes 1048576 | tf_op jit(solution)/shard_map/pallas_call | solution.py:213
  24.7 0.7 copy-done.9
  25.4 0.7 copy-done.11
  26.1 10.1 %collective-permute-done.1.refs_0_ = bf16[256,2048]{1,0:T(8,128)(2,1)} collective-permute-done((bf16[256,2048]{1,0:T(8,128)(2,1)}, bf16[256,2048]{1,0:T(8,128)(2,1)}, u32[]{:S(2)}, u32[]{:S(2)}) %collective-permute-start.1) | collective-permute-done | bytes 1048608 | tf_op jit(solution)/shard_map/ppermute | solution.py:245
  36.2 1.5 %collective-permute-start.11 = (bf16[256,2048]{1,0:T(8,128)(2,1)}, bf16[256,2048]{1,0:T(8,128)(2,1)}, u32[]{:S(2)}, u32[]{:S(2)}) collective-permute-start(bf16[256,2048]{1,0:T(8,128)(2,1)} %constant_dynamic-slice_fusion.1), channel_id=1, source_target_pairs={{0,2},{2,0},{1,3},{3,1},{4,6},{6,4},{5,7},{7,5},{8,10},{10,8},{9,1... | collective-permute-start | bytes 3145736 | tf_op jit(solution)/shard_map/ppermute | solution.py:251
  37.7 1.5 %collective-permute-start.8 = (bf16[256,2048]{1,0:T(8,128)(2,1)}, bf16[256,2048]{1,0:T(8,128)(2,1)}, u32[]{:S(2)}, u32[]{:S(2)}) collective-permute-start(bf16[256,2048]{1,0:T(8,128)(2,1)} %collective-permute-done.1.refs_0_), channel_id=1, source_target_pairs={{0,16},{16,0},{1,17},{17,1},{2,18},{18,2},{3,19},{19,3},{4,20},{20... | collective-permute-start | bytes 3145736 | tf_op jit(solution)/shard_map/ppermute | solution.py:252
  39.2 2.9 %collective-permute-start.7 = (bf16[384,2048]{1,0:T(8,128)(2,1)}, bf16[384,2048]{1,0:T(8,128)(2,1)}, u32[]{:S(2)}, u32[]{:S(2)}) collective-permute-start(bf16[384,2048]{1,0:T(8,128)(2,1)} %collective-permute-done.6.refs_0_), channel_id=1, source_target_pairs={{0,4},{4,0},{8,12},{12,8},{1,5},{5,1},{9,13},{13,9},{2,6},{6,2},{1... | collective-permute-start | bytes 4718600 | tf_op jit(solution)/shard_map/ppermute | solution.py:256
  42.1 1.8 %collective-permute-start.5 = (bf16[384,2048]{1,0:T(8,128)(2,1)}, bf16[384,2048]{1,0:T(8,128)(2,1)}, u32[]{:S(2)}, u32[]{:S(2)}) collective-permute-start(bf16[384,2048]{1,0:T(8,128)(2,1)} %collective-permute-done.refs_0_), channel_id=1, source_target_pairs={{4,8},{8,4},{5,9},{9,5},{6,10},{10,6},{7,11},{11,7},{20,24},{24,20... | collective-permute-start | bytes 4718600 | tf_op jit(solution)/shard_map/ppermute | solution.py:255
  44.0 0.9 copy-done.10
  44.9 0.9 copy-done.12
  45.8 3.4 %shard_map.57 = (f32[384,64]{1,0:T(8,128)S(1)}, f32[384,64]{1,0:T(8,128)S(1)}) custom-call(s32[1]{0:T(128)} %bitcast.6.first, bf16[256,2048]{1,0:T(8,128)(2,1)} %collective-permute-done.1.refs_0_, bf16[384,2048]{1,0:T(8,128)(2,1)S(1)} %copy-done.1, bf16[384,2048]{1,0:T(8,128)(2,1)S(1)} %collective-permute-done.2.refs_2_, ...), custom_call_target="tpu_custom_call" | custom-call | flops 161061280 | bytes 524288 | tf_op jit(solution)/shard_map/pallas_call | solution.py:213
  49.3 7.5 %shard_map.58.refs_3_ = f32[384,2048]{1,0:T(8,128)S(1)} custom-call(s32[2]{0:T(128)S(1)} %pad_add_fusion.flags, bf16[384,2048]{1,0:T(8,128)(2,1)} %collective-permute-done.refs_0_, bf16[8192,2048]{1,0:T(8,128)(2,1)} %refs_2_.1, f32[384,2048]{1,0:T(8,128)S(1)} %copy-done.5), custom_call_target="tpu_custom_call" | custom-call | flops 644245120 | bytes 2936012 | tf_op jit(solution)/shard_map/pallas_call | solution.py:67
  56.8 1.7 %copy-done.2 = f32[384,2048]{1,0:T(8,128)} copy-done((f32[384,2048]{1,0:T(8,128)}, f32[384,2048]{1,0:T(8,128)S(1)}, u32[]{:S(2)}) %copy-start.2) | copy-done | bytes 3145752
  58.5 2.8 %collective-permute-done.11.rest_1_ = bf16[256,2048]{1,0:T(8,128)(2,1)} collective-permute-done((bf16[256,2048]{1,0:T(8,128)(2,1)}, bf16[256,2048]{1,0:T(8,128)(2,1)}, u32[]{:S(2)}, u32[]{:S(2)}) %collective-permute-start.11) | collective-permute-done | bytes 1048608 | tf_op jit(solution)/shard_map/ppermute | solution.py:251
  61.3 1.5 %collective-permute-start.12 = (bf16[256,2048]{1,0:T(8,128)(2,1)}, bf16[256,2048]{1,0:T(8,128)(2,1)}, u32[]{:S(2)}, u32[]{:S(2)}) collective-permute-start(bf16[256,2048]{1,0:T(8,128)(2,1)} %collective-permute-done.11.rest_1_), channel_id=1, source_target_pairs={{0,16},{16,0},{1,17},{17,1},{2,18},{18,2},{3,19},{19,3},{4,20},{20... | collective-permute-start | bytes 3145736 | tf_op jit(solution)/shard_map/ppermute | solution.py:268
  62.8 3.3 %shard_map.59 = (f32[384,64]{1,0:T(8,128)S(1)}, f32[384,64]{1,0:T(8,128)S(1)}) custom-call(s32[1]{0:T(128)} %bitcast.5.first, bf16[256,2048]{1,0:T(8,128)(2,1)} %collective-permute-done.8.refs_0_, bf16[384,2048]{1,0:T(8,128)(2,1)S(1)} %copy-done.1, bf16[384,2048]{1,0:T(8,128)(2,1)S(1)} %collective-permute-done.2.refs_2_, ...), custom_call_target="tpu_custom_call" | custom-call | flops 161061280 | bytes 524288 | tf_op jit(solution)/shard_map/pallas_call | solution.py:213
  66.1 1.3 %collective-permute-done.9 = bf16[384,64]{1,0:T(8,128)(2,1)S(1)} collective-permute-done((bf16[384,64]{1,0:T(8,128)(2,1)S(1)}, bf16[384,64]{1,0:T(8,128)(2,1)S(1)}, u32[]{:S(2)}, u32[]{:S(2)}) %collective-permute-start.9) | collective-permute-done | bytes 49184 | tf_op jit(solution)/shard_map/ppermute | solution.py:260
  67.6 16.8 %all_to_all.5 = bf16[4,64,384]{2,1,0:T(8,128)(2,1)S(1)} all-to-all(bf16[4,64,384]{2,1,0:T(8,128)(2,1)S(1)} %broadcast_in_dim.2), channel_id=1, replica_groups=mesh['replica'=2,'tensor'=4,'adapter'=4] {'tensor'}, dimensions={0} | all-to-all | bytes 393216 | tf_op jit(solution)/shard_map/all_to_all | solution.py:263
  85.7 8.5 %constant_dynamic-slice_fusion.weight_ref = bf16[2048,2048]{1,0:T(8,128)(2,1)} fusion(bf16[8192,2048]{1,0:T(8,128)(2,1)} %refs_2_.1, s32[]{:T(128)S(6)} %select_n.23), kind=kLoop, calls=%fused_computation.2 | loop fusion | bytes 16777220 | tf_op jit(solution)/shard_map/dynamic_slice | solution.py:275
  94.2 8.1 %shard_map.60.acc_ref = f32[384,2048]{1,0:T(8,128)S(1)} custom-call(s32[2]{0:T(128)S(1)} %pad_add_fusion.2.flags, bf16[384,2048]{1,0:T(8,128)(2,1)} %collective-permute-done.6.refs_0_, bf16[384,2048]{1,0:T(8,128)(2,1)} %collective-permute-done.7.refs_1_, bf16[8192,2048]{1,0:T(8,128)(2,1)} %refs_2_.1, f32[384,2048]{1,0:T(8,128)S(1)} %copy-done.3), custom_call_target="tpu_custom_call" | custom-call | flops 644245120 | bytes 2936012 | tf_op jit(solution)/shard_map/pallas_call | solution.py:67
  102.3 7.4 %shard_map.61.acc_ref = f32[384,2048]{1,0:T(8,128)S(1)} custom-call(s32[6]{0:T(128)S(1)} %stack.43.firsts, bf16[384,64]{1,0:T(8,128)(2,1)S(1)} %bitcast.20, s32[384,1]{1,0:T(8,128)S(1)} %copy.13.refs_3_.owner_ref, f32[384,2048]{1,0:T(8,128)S(1)} %shard_map.60.acc_ref, bf16[512,2048]{1,0:T(8,128)(2,1)S(1)} %bitcast.19, ...), custom_call_target="tpu_custom_call" | custom-call | flops 644245120 | bytes 2936012 | tf_op jit(solution)/shard_map/pallas_call | solution.py:165
  109.8 9.1 %collective-permute-done.10.there = bf16[384,2048]{1,0:T(8,128)(2,1)S(1)} collective-permute-done((bf16[384,2048]{1,0:T(8,128)(2,1)}, bf16[384,2048]{1,0:T(8,128)(2,1)S(1)}, u32[]{:S(2)}, u32[]{:S(2)}) %collective-permute-start.10) | collective-permute-done | bytes 1572896 | tf_op jit(solution)/shard_map/ppermute | solution.py:266
  118.9 4.5 %shard_map.62 = bf16[384,2048]{1,0:T(8,128)(2,1)} custom-call(s32[1]{0:T(128)} %bitcast.inner, bf16[384,2048]{1,0:T(8,128)(2,1)} %collective-permute-done.5.here, bf16[384,2048]{1,0:T(8,128)(2,1)S(1)} %collective-permute-done.10.there, bf16[2048,2048]{1,0:T(8,128)(2,1)S(1)} %copy-done, f32[384,2048]{1,0:T(8,128)S(1)} %shard_map.61.acc_ref), custom_call_target="tpu_custom_call" | custom-call | flops 644245120 | bytes 2936012 | tf_op jit(solution)/shard_map/pallas_call | solution.py:115
  (47 shorter events, 2.3 us)
Async XLA Ops:
  0.0 11.9 %copy-start.1 = (bf16[384,2048]{1,0:T(8,128)(2,1)S(1)}, bf16[384,2048]{1,0:T(8,128)(2,1)}, u32[]{:S(2)}) copy-start(bf16[384,2048]{1,0:T(8,128)(2,1)} %refs_1_.9) | copy-start | bytes 4718596
  0.0 36.2 %collective-permute-start.4 = (bf16[512,2048]{1,0:T(8,128)(2,1)}, bf16[512,2048]{1,0:T(8,128)(2,1)}, u32[]{:S(2)}, u32[]{:S(2)}) collective-permute-start(bf16[512,2048]{1,0:T(8,128)(2,1)} %bitcast.17), channel_id=1, source_target_pairs={{0,1},{1,0},{2,3},{3,2},{4,5},{5,4},{6,7},{7,6},{8,9},{9,8},{10,11... | collective-permute-start | bytes 6291464 | tf_op jit(solution)/shard_map/ppermute | solution.py:246
  0.5 21.2 %collective-permute-start.2 = (bf16[384,2048]{1,0:T(8,128)(2,1)}, bf16[384,2048]{1,0:T(8,128)(2,1)S(1)}, u32[]{:S(2)}, u32[]{:S(2)}) collective-permute-start(bf16[384,2048]{1,0:T(8,128)(2,1)} %refs_1_.9), channel_id=1, source_target_pairs={{0,1},{1,0},{2,3},{3,2},{4,5},{5,4},{6,7},{7,6},{8,9},{9,8},{10,11... | collective-permute-start | bytes 4718600 | tf_op jit(solution)/shard_map/ppermute | solution.py:243
  0.5 38.7 %collective-permute-start.6 = (bf16[384,2048]{1,0:T(8,128)(2,1)}, bf16[384,2048]{1,0:T(8,128)(2,1)}, u32[]{:S(2)}, u32[]{:S(2)}) collective-permute-start(bf16[384,2048]{1,0:T(8,128)(2,1)} %refs_1_.9), channel_id=1, source_target_pairs={{4,8},{8,4},{5,9},{9,5},{6,10},{10,6},{7,11},{11,7},{20,24},{24,20... | collective-permute-start | bytes 4718600 | tf_op jit(solution)/shard_map/ppermute | solution.py:241
  2.3 39.8 %collective-permute-start = (bf16[384,2048]{1,0:T(8,128)(2,1)}, bf16[384,2048]{1,0:T(8,128)(2,1)}, u32[]{:S(2)}, u32[]{:S(2)}) collective-permute-start(bf16[384,2048]{1,0:T(8,128)(2,1)} %refs_1_.9), channel_id=1, source_target_pairs={{0,4},{4,0},{8,12},{12,8},{1,5},{5,1},{9,13},{13,9},{2,6},{6,2},{1... | collective-permute-start | bytes 4718600 | tf_op jit(solution)/shard_map/ppermute | solution.py:240
  7.9 2.4 %collective-permute-start.3 = (s32[384,1]{1,0:T(8,128)S(1)}, s32[384,1]{1,0:T(8,128)S(1)}, u32[]{:S(2)}, u32[]{:S(2)}) collective-permute-start(s32[384,1]{1,0:T(8,128)S(1)} %copy.13.refs_3_.owner_ref), channel_id=1, source_target_pairs={{0,1},{1,0},{2,3},{3,2},{4,5},{5,4},{6,7},{7,6},{8,9},{9,8},{10,11... | collective-permute-start | bytes 4616 | tf_op jit(solution)/shard_map/ppermute | solution.py:244
  10.3 25.9 %collective-permute-start.1 = (bf16[256,2048]{1,0:T(8,128)(2,1)}, bf16[256,2048]{1,0:T(8,128)(2,1)}, u32[]{:S(2)}, u32[]{:S(2)}) collective-permute-start(bf16[256,2048]{1,0:T(8,128)(2,1)} %constant_dynamic-slice_fusion.2), channel_id=1, source_target_pairs={{0,2},{2,0},{1,3},{3,1},{4,6},{6,4},{5,7},{7,5},{8,10},{10,8},{9,1... | collective-permute-start | bytes 3145736 | tf_op jit(solution)/shard_map/ppermute | solution.py:245
  11.9 8.7 %copy-start.7 = (bf16[8,64,2048]{2,1,0:T(8,128)(2,1)S(1)}, bf16[8,64,2048]{2,1,0:T(8,128)(2,1)}, u32[]{:S(2)}) copy-start(bf16[8,64,2048]{2,1,0:T(8,128)(2,1)} %param.8) | copy-start | bytes 6291460
  18.9 1.6 %copy-start.4 = (f32[384,2048]{1,0:T(8,128)}, f32[384,2048]{1,0:T(8,128)S(1)}, u32[]{:S(2)}) copy-start(f32[384,2048]{1,0:T(8,128)S(1)} %shard_map.55.refs_2_) | copy-start | bytes 9437188
  20.5 2.0 %copy-start.6 = (bf16[8,64,2048]{2,1,0:T(8,128)(2,1)S(1)}, bf16[8,64,2048]{2,1,0:T(8,128)(2,1)}, u32[]{:S(2)}) copy-start(bf16[8,64,2048]{2,1,0:T(8,128)(2,1)} %param.7) | copy-start | bytes 6291460
  24.7 0.7 copy-start.9
  25.4 0.7 copy-start.11
  36.2 25.1 %collective-permute-start.11 = (bf16[256,2048]{1,0:T(8,128)(2,1)}, bf16[256,2048]{1,0:T(8,128)(2,1)}, u32[]{:S(2)}, u32[]{:S(2)}) collective-permute-start(bf16[256,2048]{1,0:T(8,128)(2,1)} %constant_dynamic-slice_fusion.1), channel_id=1, source_target_pairs={{0,2},{2,0},{1,3},{3,1},{4,6},{6,4},{5,7},{7,5},{8,10},{10,8},{9,1... | collective-permute-start | bytes 3145736 | tf_op jit(solution)/shard_map/ppermute | solution.py:251
  37.7 25.1 %collective-permute-start.8 = (bf16[256,2048]{1,0:T(8,128)(2,1)}, bf16[256,2048]{1,0:T(8,128)(2,1)}, u32[]{:S(2)}, u32[]{:S(2)}) collective-permute-start(bf16[256,2048]{1,0:T(8,128)(2,1)} %collective-permute-done.1.refs_0_), channel_id=1, source_target_pairs={{0,16},{16,0},{1,17},{17,1},{2,18},{18,2},{3,19},{19,3},{4,20},{20... | collective-permute-start | bytes 3145736 | tf_op jit(solution)/shard_map/ppermute | solution.py:252
  39.2 45.4 %collective-permute-start.7 = (bf16[384,2048]{1,0:T(8,128)(2,1)}, bf16[384,2048]{1,0:T(8,128)(2,1)}, u32[]{:S(2)}, u32[]{:S(2)}) collective-permute-start(bf16[384,2048]{1,0:T(8,128)(2,1)} %collective-permute-done.6.refs_0_), channel_id=1, source_target_pairs={{0,4},{4,0},{8,12},{12,8},{1,5},{5,1},{9,13},{13,9},{2,6},{6,2},{1... | collective-permute-start | bytes 4718600 | tf_op jit(solution)/shard_map/ppermute | solution.py:256
  42.1 42.5 %collective-permute-start.5 = (bf16[384,2048]{1,0:T(8,128)(2,1)}, bf16[384,2048]{1,0:T(8,128)(2,1)}, u32[]{:S(2)}, u32[]{:S(2)}) collective-permute-start(bf16[384,2048]{1,0:T(8,128)(2,1)} %collective-permute-done.refs_0_), channel_id=1, source_target_pairs={{4,8},{8,4},{5,9},{9,5},{6,10},{10,6},{7,11},{11,7},{20,24},{24,20... | collective-permute-start | bytes 4718600 | tf_op jit(solution)/shard_map/ppermute | solution.py:255
  44.0 0.9 copy-start.10
  44.9 0.9 copy-start.12
  45.8 3.4 %copy-start.5 = (f32[384,2048]{1,0:T(8,128)S(1)}, f32[384,2048]{1,0:T(8,128)}, u32[]{:S(2)}) copy-start(f32[384,2048]{1,0:T(8,128)} %copy-done.4) | copy-start | bytes 9437188
  56.8 1.7 %copy-start.2 = (f32[384,2048]{1,0:T(8,128)}, f32[384,2048]{1,0:T(8,128)S(1)}, u32[]{:S(2)}) copy-start(f32[384,2048]{1,0:T(8,128)S(1)} %shard_map.58.refs_3_) | copy-start | bytes 9437188
  61.3 24.2 %collective-permute-start.12 = (bf16[256,2048]{1,0:T(8,128)(2,1)}, bf16[256,2048]{1,0:T(8,128)(2,1)}, u32[]{:S(2)}, u32[]{:S(2)}) collective-permute-start(bf16[256,2048]{1,0:T(8,128)(2,1)} %collective-permute-done.11.rest_1_), channel_id=1, source_target_pairs={{0,16},{16,0},{1,17},{17,1},{2,18},{18,2},{3,19},{19,3},{4,20},{20... | collective-permute-start | bytes 3145736 | tf_op jit(solution)/shard_map/ppermute | solution.py:268
  66.1 1.4 %collective-permute-start.9 = (bf16[384,64]{1,0:T(8,128)(2,1)S(1)}, bf16[384,64]{1,0:T(8,128)(2,1)S(1)}, u32[]{:S(2)}, u32[]{:S(2)}) collective-permute-start(bf16[384,64]{1,0:T(8,128)(2,1)S(1)} %convert_element_type.16), channel_id=1, source_target_pairs={{0,1},{1,0},{2,3},{3,2},{4,5},{5,4},{6,7},{7,6},{8,9},{9,8},{10,11... | collective-permute-start | bytes 147464 | tf_op jit(solution)/shard_map/ppermute | solution.py:260
  84.6 34.3 %collective-permute-start.10 = (bf16[384,2048]{1,0:T(8,128)(2,1)}, bf16[384,2048]{1,0:T(8,128)(2,1)S(1)}, u32[]{:S(2)}, u32[]{:S(2)}) collective-permute-start(bf16[384,2048]{1,0:T(8,128)(2,1)} %collective-permute-done.5.here), channel_id=1, source_target_pairs={{0,4},{4,0},{8,12},{12,8},{1,5},{5,1},{9,13},{13,9},{2,6},{6,2},{1... | collective-permute-start | bytes 4718600 | tf_op jit(solution)/shard_map/ppermute | solution.py:266
  85.1 17.2 %collective-permute-start.13 = (bf16[256,2048]{1,0:T(8,128)(2,1)}, bf16[256,2048]{1,0:T(8,128)(2,1)S(1)}, u32[]{:S(2)}, u32[]{:S(2)}) collective-permute-start(bf16[256,2048]{1,0:T(8,128)(2,1)} %collective-permute-done.11.rest_1_), channel_id=1, source_target_pairs={{0,1},{1,0},{2,3},{3,2},{4,5},{5,4},{6,7},{7,6},{8,9},{9,8},{10,11... | collective-permute-start | bytes 3145736 | tf_op jit(solution)/shard_map/ppermute | solution.py:270
  85.5 16.9 %collective-permute-start.14 = (bf16[256,2048]{1,0:T(8,128)(2,1)}, bf16[256,2048]{1,0:T(8,128)(2,1)}, u32[]{:S(2)}, u32[]{:S(2)}) collective-permute-start(bf16[256,2048]{1,0:T(8,128)(2,1)} %collective-permute-done.12.rest_2_), channel_id=1, source_target_pairs={{0,1},{1,0},{2,3},{3,2},{4,5},{5,4},{6,7},{7,6},{8,9},{9,8},{10,11... | collective-permute-start | bytes 3145736 | tf_op jit(solution)/shard_map/ppermute | solution.py:270
  85.7 8.5 %copy-start.3 = (f32[384,2048]{1,0:T(8,128)S(1)}, f32[384,2048]{1,0:T(8,128)}, u32[]{:S(2)}) copy-start(f32[384,2048]{1,0:T(8,128)} %copy-done.2) | copy-start | bytes 9437188
  94.2 8.1 %copy-start.8 = (bf16[8,64,2048]{2,1,0:T(8,128)(2,1)S(1)}, bf16[8,64,2048]{2,1,0:T(8,128)(2,1)}, u32[]{:S(2)}) copy-start(bf16[8,64,2048]{2,1,0:T(8,128)(2,1)} %param.8) | copy-start | bytes 6291460
  102.3 16.5 %copy-start = (bf16[2048,2048]{1,0:T(8,128)(2,1)S(1)}, bf16[2048,2048]{1,0:T(8,128)(2,1)}, u32[]{:S(2)}) copy-start(bf16[2048,2048]{1,0:T(8,128)(2,1)} %constant_dynamic-slice_fusion.weight_ref) | copy-start | bytes 25165828
